TPU v7x, 32 devices: a whole 2x2x4 slice. The times are simulated.
32 devices in a mesh: row: 4 (over z), col: 8 (over y, x, core).
Axes of the slice: x: 2, y: 2, z: 4, core: 2. Of those that a mesh axis runs over, the one named last changes fastest.
Arguments:
- factor_inverse: bfloat16 [2048, 2048], P(('row', 'col')), as said below
- panel_left: float32 [16384, 256], P(('row', 'col')), may hold values from -6 to 6
- panel_right: float32 [16384, 256], P(('row', 'col')), may hold values from -12 to 12
- panel_rank: int32 [8], P('row'), may hold values from 16 to 256, as said below
- left: float32 [16384, 2048], P('row', 'col'), may hold values from -6 to 6
- right: float32 [16384, 2048], P('row', 'col'), may hold values from -6 to 6
- probes: float32 [16384, 2048], P('row', 'col'), may hold values from -6 to 6
- trail_rank: int32 [8, 8], P('row', 'col'), may hold values from 16 to 256, as said below
Outputs:
- new_left: float32 [16384, 2048], P('row', 'col')
- new_right: float32 [16384, 2048], P('row', 'col')
Inputs may be any that keep to these rules, and one draw needn't show every extreme that they name: `factor_inverse`: lower triangular with a positive diagonal. `panel_rank`: every rank is a multiple of 16, and some panel tile has rank 256. `trail_rank`: every rank is a multiple of 16, and some trailing tile has rank 256.
All inputs are finite; a program needn't handle non-finite values.
Results may differ from a plain program's by a relative error of at most 0.0012.
Values may be sent and summed in bfloat16 or wider, within the bound.
No kernel may reach another device: no remote copies, remote signals or barrier semaphores. Data moves between devices by JAX's collectives and lax.ppermute only.
A program may use at most 128 MiB of HBM per device.

v0:
```python
import math

import jax
import jax.numpy as jnp
from jax import lax
from jax.experimental import pallas as pl
from jax.experimental.pallas import tpu as pltpu
from jax.sharding import PartitionSpec as P

highest = lax.Precision.HIGHEST
SUB = 8


def split_three(x):
    a = x.astype(jnp.bfloat16)
    r = x - a.astype(jnp.float32)
    b = r.astype(jnp.bfloat16)
    c = (r - b.astype(jnp.float32)).astype(jnp.bfloat16)
    return a, b, c


def hot_dot(x, y, dims):
    return lax.dot_general(x, y, (dims, ((), ())), precision=lax.Precision.HIGHEST, preferred_element_type=jnp.float32)


def factor_blocks(block, scratch):
    count = len(block)
    n = block[0].shape[0]
    wide = 2 * n
    groups = n // SUB
    lane = lax.broadcasted_iota(jnp.int32, (SUB, wide), 1)
    sub = lax.broadcasted_iota(jnp.int32, (SUB, wide), 0)
    state = []
    for t in range(count):
        eye = [jnp.where(lane - n == sub + SUB * g, 1.0, 0.0) for g in range(groups)]
        full = jnp.concatenate([block[t], jnp.zeros((n, n), jnp.float32)], axis=1)
        state.append([full[SUB * g : SUB * (g + 1)] + eye[g] for g in range(groups)])
    out = [[None] * groups for _ in range(count)]
    for k in range(groups):
        for t in range(count):
            rows = state[t]
            spread = [
                [jnp.broadcast_to(rows[g][:, SUB * k + j : SUB * k + j + 1], (SUB, wide)) for j in range(SUB)]
                for g in range(k, groups)
            ]
            for j in range(SUB):
                scratch[t, j] = spread[0][j]
            scratch[t, SUB] = rows[k]
            a = [
                [jnp.broadcast_to(scratch[t, j, i : i + 1, :], (SUB, wide)) for j in range(i + 1)]
                for i in range(SUB)
            ]
            row = [jnp.broadcast_to(scratch[t, SUB, i : i + 1, :], (SUB, wide)) for i in range(SUB)]
            inv = [None] * SUB
            low = [[None] * SUB for _ in range(SUB)]
            for j in range(SUB):
                inv[j] = 1.0 / a[j][j]
                for i in range(j + 1, SUB):
                    low[i][j] = a[i][j] * inv[j]
                for i in range(j + 1, SUB):
                    for h in range(i, SUB):
                        a[h][i] = a[h][i] - low[h][j] * a[i][j]
                    row[i] = row[i] - low[i][j] * row[j]
            done = row[0] * lax.rsqrt(a[0][0])
            for i in range(1, SUB):
                done = jnp.where(sub == i, row[i] * lax.rsqrt(a[i][i]), done)
            out[t][k] = done
            for g in range(k + 1, groups):
                cols = spread[g - k]
                scaled = []
                value = rows[g]
                for j in range(SUB):
                    x = cols[j]
                    for h in range(j):
                        x = x - scaled[h] * a[j][h]
                    scaled.append(x * inv[j])
                    value = value - scaled[j] * row[j]
                rows[g] = value
    return [jnp.concatenate(o, axis=0)[:, n:] for o in out]


def inverse_factor(gram_of, put, order, step, scratch, count):
    work = [gram_of(t) for t in range(count)]
    eye = (
        lax.broadcasted_iota(jnp.int32, (order, order), 0) == lax.broadcasted_iota(jnp.int32, (order, order), 1)
    )
    scale = []
    for t in range(count):
        diag = jnp.where(eye, work[t], 0.0)
        down = lax.rsqrt(jnp.sum(diag, axis=1, keepdims=True))
        across = lax.rsqrt(jnp.sum(diag, axis=0, keepdims=True))
        scale.append(across)
        work[t] = jnp.concatenate([work[t] * down * across, jnp.where(eye, 1.0, 0.0)], axis=1)
    for k in range(order // step):
        lo = k * step
        inner = factor_blocks([w[:step, lo : lo + step] for w in work], scratch)
        for t in range(count):
            solved = hot_dot(inner[t], work[t][:step], ((1,), (0,)))
            put(t, lo, solved[:, order:] * scale[t])
            if lo + step < order:
                tail = solved[:, lo + step : order]
                work[t] = work[t][step:] - hot_dot(tail, solved, ((0,), (0,)))


def factor_kernel(gram_ref, out_ref, scratch):
    count, order, _ = gram_ref.shape

    def put(t, lo, value):
        out_ref[t, lo : lo + value.shape[0], :] = value

    inverse_factor(lambda t: gram_ref[t], put, order, 64, scratch, count)


def factor(gram, **kw):
    return pl.pallas_call(
        factor_kernel,
        out_shape=jax.ShapeDtypeStruct(gram.shape, jnp.float32),
        in_specs=[pl.BlockSpec(memory_space=pltpu.VMEM)],
        out_specs=pl.BlockSpec(memory_space=pltpu.VMEM),
        scratch_shapes=[pltpu.VMEM((gram.shape[0], SUB + 1, SUB, 128), jnp.float32)],
        compiler_params=pltpu.CompilerParams(vmem_limit_bytes=32 * 1024 * 1024),
        **kw,
    )(gram)


def flip(value, axis, size, mask):
    return lax.ppermute(value, axis, [(i, i ^ mask) for i in range(size)])


def dot(spec, a, b):
    return jnp.einsum(spec, a, b, precision=highest, preferred_element_type=jnp.float32)


def call(kernel, out, args, kinds, scratch=(), limit=40):
    spaces = {"v": pltpu.VMEM, "s": pltpu.SMEM, "a": pl.ANY}
    flat = jax.tree.leaves(out)
    shapes = [jax.ShapeDtypeStruct(s.shape, s.dtype) for s in flat]
    where = pl.ANY if kinds[-1] == "a" else pltpu.VMEM
    result = pl.pallas_call(
        kernel,
        out_shape=shapes,
        in_specs=[pl.BlockSpec(memory_space=spaces[k]) for k in kinds[:-1]],
        out_specs=[pl.BlockSpec(memory_space=where)] * len(shapes),
        scratch_shapes=list(scratch),
        compiler_params=pltpu.CompilerParams(vmem_limit_bytes=limit * 1024 * 1024),
    )(*args)
    return result


def shaped(shape, dtype=jnp.float32):
    return jax.ShapeDtypeStruct(shape, dtype)


def solve_kernel(rows, pairs, where_ref, rank_ref, *refs):
    inverse, held, other = refs[:rows], refs[rows : rows + pairs], refs[rows + pairs]
    out_ref, whole = refs[rows + pairs + 1 :]
    floor, me = where_ref[0], where_ref[1]
    part = inverse[0].shape[0]
    chunk, cap = held[0].shape
    quarters = pairs
    half, quarter = me // quarters, me % quarters
    for d in range(rows):
        whole[pl.ds(pl.multiple_of((floor ^ d) * part, part), part), :] = inverse[d][...]
    column = lax.broadcasted_iota(jnp.int32, (1, cap), 1)
    for h in range(2):
        total = None
        for d in range(quarters):
            at = h * quarters + d
            value = held[at // 2][...] if at % 2 == 0 else other[at // 2]
            lhs = whole[:, pl.ds(pl.multiple_of((quarter ^ d) * chunk, chunk), chunk)]
            for piece in split_three(value):
                term = jnp.dot(lhs, piece, preferred_element_type=jnp.float32)
                total = term if total is None else total + term
        tile = half ^ h
        kept = column < rank_ref[tile]
        out_ref[:, pl.ds(pl.multiple_of(tile * cap, cap), cap)] = jnp.where(kept, total, 0.0)


def core_kernel(rows, pairs, where_ref, *refs):
    solved, (mine_ref, theirs_ref) = refs[:rows], refs[rows:]
    floor, me = where_ref[0], where_ref[1]
    pair, side = me // 2, me % 2
    cap = mine_ref.shape[2]
    own = solved[0][...]
    own_high = own.astype(jnp.bfloat16)
    own_low = (own - own_high.astype(jnp.float32)).astype(jnp.bfloat16)

    def across(x, y):
        return lax.dot_general(x, y, (((0,), (0,)), ((), ())), preferred_element_type=jnp.float32)

    for e in range(pairs):
        wanted = floor ^ pair ^ e
        value = own
        for d in range(1, rows):
            value = jnp.where(wanted == d, solved[d][...], value)
        high = value.astype(jnp.bfloat16)
        low = (value - high.astype(jnp.float32)).astype(jnp.bfloat16)
        part = across(own_high, high) + (across(own_high, low) + across(own_low, high))
        left, right = part[:, :cap], part[:, cap:]
        mine_ref[e] = jnp.where(side == 0, left, right)
        theirs_ref[e] = jnp.where(side == 0, right, left)


def place_kernel(count, slot_ref, *refs):
    blocks, out_ref, sem = refs[: -2], refs[-2], refs[-1]
    flat = []
    for b in blocks:
        flat += [b] if len(b.shape) == 2 else [b.at[i] for i in range(b.shape[0])]
    copies = []
    for n in range(count):
        chunk = flat[n].shape[0]
        at = pl.multiple_of(slot_ref[n] * chunk, chunk)
        copies.append(pltpu.make_async_copy(flat[n], out_ref.at[pl.ds(at, chunk)], sem.at[n]))
    for c in copies:
        c.start()
    for c in copies:
        c.wait()


def place(slots, blocks, count):
    chunk, width = blocks[0].shape[-2:]
    return call(
        lambda *refs: place_kernel(count, *refs),
        [shaped((count * chunk, width))],
        [jnp.stack(slots), *blocks],
        "s" + "a" * (len(blocks) + 1),
        [pltpu.SemaphoreType.DMA((count,))],
    )[0]


def make_shards(rows, cols):
    pairs = cols // 2

    def shards(factor_inverse, panel_left, panel_right, panel_rank, left, right, probes, trail_rank):
        tile_rows, tile_cols = trail_rank.shape
        tile_order = factor_inverse.shape[1]
        rank_cap = left.shape[1] // tile_cols
        chunk = panel_left.shape[0]
        part = factor_inverse.shape[0]
        root_width = math.sqrt(tile_order)
        me = lax.axis_index("col").astype(jnp.int32)
        floor = lax.axis_index("row").astype(jnp.int32)
        spot = jnp.stack([floor, me])
        columns = jnp.arange(rank_cap, dtype=jnp.int32)
        my_pair, my_side = me // 2, me % 2

        def row_gather(block):
            held = [block] + [flip(block, "col", cols, 2 * d) for d in range(1, pairs)]
            return held, flip(jnp.stack(held), "col", cols, 1)

        inverse = [factor_inverse] + [flip(factor_inverse, "row", rows, d) for d in range(1, rows)]
        slices = lax.all_gather(panel_left, "row", axis=0)
        held, other = row_gather(panel_right)
        solved = call(
            lambda *refs: solve_kernel(rows, pairs, *refs),
            [shaped((rows * part, tile_rows * rank_cap))],
            [spot, panel_rank, *inverse, *held, other],
            "ss" + "v" * (rows + pairs + 2),
            [pltpu.VMEM((rows * part, tile_order), jnp.bfloat16)],
        )[0]
        all_solved = [solved] + [flip(solved, "row", rows, d) for d in range(1, rows)]

        held, other = row_gather(panel_left)
        row_left = place([me ^ (2 * d) for d in range(pairs)] + [me ^ (2 * d + 1) for d in range(pairs)], [*held, other], cols)
        row_left = row_left.reshape(tile_rows, tile_order, rank_cap)

        got = [lax.dynamic_index_in_dim(slices, my_pair ^ d, 0, keepdims=False) for d in range(pairs)]
        got = [flip(got[d], "col", cols, 2 * d) if d else got[d] for d in range(pairs)]
        half = pairs // 2
        top = my_pair // half
        upper = (top ^ my_side) == 1
        keep = [jnp.where(upper, got[half + d], got[d]) for d in range(half)]
        give = [jnp.where(upper, got[d], got[half + d]) for d in range(half)]
        take = flip(jnp.stack(give), "col", cols, 1)
        low = my_pair % half
        col_left = place(
            [2 * (low ^ d) + my_side for d in range(half)] + [2 * (low ^ d) + 1 - my_side for d in range(half)],
            [*keep, take],
            pairs,
        )

        mine, theirs = call(
            lambda *refs: core_kernel(rows, pairs, *refs),
            [shaped((pairs, tile_rows * rank_cap, rank_cap))] * 2,
            [spot, *all_solved],
            "s" + "v" * (rows + 1),
        )
        theirs = flip(theirs, "col", cols, 1)
        parts = [mine[e] + theirs[e] for e in range(pairs)]
        panel_core = sum(flip(parts[e], "col", cols, 2 * e) if e else parts[e] for e in range(pairs))
        panel_core = panel_core.reshape(tile_rows, rank_cap, rank_cap) / tile_order

        kept_cols = (columns[None, :] < trail_rank).astype(jnp.float32)[:, None, :]

        def to_tiles(block):
            return block.reshape(tile_rows, tile_order, rank_cap) * kept_cols

        tile_left = to_tiles(left)
        tile_right = to_tiles(right)
        tile_probe = to_tiles(probes)
        right_probe = dot("tnk,tnl->tkl", tile_right, tile_probe)
        tile_part = dot("tnk,tkl->tnl", tile_left, right_probe)
        panel_probe = dot("nk,tnl->tkl", col_left, tile_probe)
        core_probe = dot("tkl,tlm->tkm", panel_core, panel_probe)
        sampled = (tile_part - dot("tnk,tkl->tnl", row_left, core_probe)) / tile_order
        identity = (columns[:, None] == columns[None, :]).astype(jnp.float32)
        gram_matrix = dot("tnk,tnl->tkl", sampled, sampled)
        gram_matrix = gram_matrix + (1.0 - kept_cols) * identity
        inverse_gram = factor(gram_matrix)
        new_basis = dot("tnk,tlk->tnl", sampled, inverse_gram) * root_width
        left_proj = dot("tnk,tnl->tkl", tile_left, new_basis)
        panel_proj = dot("tnk,tnl->tkl", row_left, new_basis)
        core_proj = dot("tlk,tlm->tkm", panel_core, panel_proj)
        new_factor = (
            dot("tnk,tkl->tnl", tile_right, left_proj) - dot("nk,tkl->tnl", col_left, core_proj)
        ) / tile_order
        return (
            new_basis.reshape(tile_rows * tile_order, rank_cap),
            new_factor.reshape(tile_rows * tile_order, rank_cap),
        )

    return shards


def solution(mesh):
    return jax.shard_map(
        make_shards(mesh.shape["row"], mesh.shape["col"]),
        mesh=mesh,
        in_specs=(
            P(("row", "col"), None),
            P(("row", "col"), None),
            P(("row", "col"), None),
            P("row"),
            P("row", "col"),
            P("row", "col"),
            P("row", "col"),
            P("row", "col"),
        ),
        out_specs=(P("row", "col"), P("row", "col")),
        check_vma=False,
    )
```

profile of v0, /device:TPU:0, one launch (start us, length us, event | category | flops | bytes accessed | tf_op | source)
XLA Modules:
  0.0 273.4 jit_solution(11742915478563969323)
XLA Ops:
  7.2 4.0 %collective-permute-start.9 = (f32[512,256]{1,0:T(8,128)}, f32[512,256]{1,0:T(8,128)S(1)}, u32[]{:S(2)}, u32[]{:S(2)}) collective-permute-start(f32[512,256]{1,0:T(8,128)} %refs_6_.1), channel_id=1, source_target_pairs={{0,6},{1,7},{2,4},{3,5},{4,2},{5,3},{6,0},{7,1},{8,14},{9,15},{10,... | collective-permute-start | bytes 1572872 | tf_op jit(solution)/shard_map/ppermute | solution.py:127
  11.9 12.3 %collective-permute-done.9.refs_9_ = f32[512,256]{1,0:T(8,128)S(1)} collective-permute-done((f32[512,256]{1,0:T(8,128)}, f32[512,256]{1,0:T(8,128)S(1)}, u32[]{:S(2)}, u32[]{:S(2)}) %collective-permute-start.9) | collective-permute-done | bytes 524320 | tf_op jit(solution)/shard_map/ppermute | solution.py:127
  24.2 10.4 %collective-permute-done.8.refs_8_ = f32[512,256]{1,0:T(8,128)S(1)} collective-permute-done((f32[512,256]{1,0:T(8,128)}, f32[512,256]{1,0:T(8,128)S(1)}, u32[]{:S(2)}, u32[]{:S(2)}) %collective-permute-start.8) | collective-permute-done | bytes 524320 | tf_op jit(solution)/shard_map/ppermute | solution.py:127
  34.9 2.6 pad_maximum_fusion.1
  39.8 2.6 collective-permute-start.5
  44.3 22.5 %collective-permute-done.5.refs_4_ = bf16[64,2048]{1,0:T(8,128)(2,1)S(1)} collective-permute-done((bf16[64,2048]{1,0:T(8,128)(2,1)S(1)}, bf16[64,2048]{1,0:T(8,128)(2,1)S(1)}, u32[]{:S(2)}, u32[]{:S(2)}) %collective-permute-start.5) | collective-permute-done | bytes 262176 | tf_op jit(solution)/shard_map/ppermute | solution.py:127
  68.2 8.4 %collective-permute-done.6.refs_5_ = bf16[64,2048]{1,0:T(8,128)(2,1)} collective-permute-done((bf16[64,2048]{1,0:T(8,128)(2,1)S(1)}, bf16[64,2048]{1,0:T(8,128)(2,1)}, u32[]{:S(2)}, u32[]{:S(2)}) %collective-permute-start.6) | collective-permute-done | bytes 262176 | tf_op jit(solution)/shard_map/ppermute | solution.py:127
  82.7 3.0 %shard_map.96.refs_1_ = f32[256,512]{1,0:T(8,128)S(1)} custom-call(s32[2]{0:T(128)S(1)} %pad_add_fusion.refs_0_, s32[2]{0:T(128)S(1)} %copy-done.17, bf16[64,2048]{1,0:T(8,128)(2,1)S(1)} %copy-done.12, bf16[64,2048]{1,0:T(8,128)(2,1)S(1)} %copy-done.16, bf16[64,2048]{1,0:T(8,128)(2,1)S(1)} %copy-done.14, bf16[64,2048]{1,0:T(8,128)(2,1)} %collective-permute-done.6.refs_5_, ...), custom_call_target="tpu_custom_call" | custom-call | tf_op jit(solution)/shard_map/pallas_call | solution.py:139
  86.2 6.6 %collective-permute-start.12 = (f32[256,512]{1,0:T(8,128)S(1)}, f32[256,512]{1,0:T(8,128)}, u32[]{:S(2)}, u32[]{:S(2)}) collective-permute-start(f32[256,512]{1,0:T(8,128)S(1)} %shard_map.96.refs_1_), channel_id=1, source_target_pairs={{0,16},{8,24},{16,0},{24,8},{1,17},{9,25},{17,1},{25,9},{2,18},{10... | collective-permute-start | bytes 1572872 | tf_op jit(solution)/shard_map/ppermute | solution.py:127
  92.8 2.4 collective-permute-start.2
  95.8 6.7 %collective-permute-done.13.refs_4_ = f32[256,512]{1,0:T(8,128)S(1)} collective-permute-done((f32[256,512]{1,0:T(8,128)S(1)}, f32[256,512]{1,0:T(8,128)S(1)}, u32[]{:S(2)}, u32[]{:S(2)}) %collective-permute-start.13) | collective-permute-done | bytes 524320 | tf_op jit(solution)/shard_map/ppermute | solution.py:127
  104.0 31.1 %collective-permute-done.12.refs_3_ = f32[256,512]{1,0:T(8,128)} collective-permute-done((f32[256,512]{1,0:T(8,128)S(1)}, f32[256,512]{1,0:T(8,128)}, u32[]{:S(2)}, u32[]{:S(2)}) %collective-permute-start.12) | collective-permute-done | bytes 524320 | tf_op jit(solution)/shard_map/ppermute | solution.py:127
  135.1 4.5 %shard_map.97 = (f32[4,512,256]{2,1,0:T(8,128)S(1)}, f32[4,512,256]{2,1,0:T(8,128)}) custom-call(s32[2]{0:T(128)S(1)} %pad_add_fusion.refs_0_, f32[256,512]{1,0:T(8,128)S(1)} %shard_map.96.refs_1_, f32[256,512]{1,0:T(8,128)} %collective-permute-done.11.refs_2_, f32[256,512]{1,0:T(8,128)} %collective-permute-done.12.refs_3_, ...), custom_call_target="tpu_custom_call" | custom-call | tf_op jit(solution)/shard_map/pallas_call | solution.py:139
  140.9 1.6 dynamic-slice_bitcast_fusion
  147.9 9.0 %fusion.3 = f32[2,256,256]{2,1,0:T(8,128)S(1)} fusion(f32[2,2048,256]{2,1,0:T(8,128)S(1)} %bitcast.99, f32[2,2048,256]{2,1,0:T(8,128)} %bitcast.101, f32[2,256]{1,0:T(2,128)S(1)} %compare_convert_fusion), kind=kOutput, calls=%fused_computation.5 | convolution fusion | flops 3223322624 | bytes 8914944 | tf_op jit(solution)/shard_map/tnk,tnl->tkl/dot_general | solution.py:131
  158.1 2.5 collective-permute-done.20
  160.5 10.7 %collective-permute-done.19 = f32[512,256]{1,0:T(8,128)S(1)} collective-permute-done((f32[512,256]{1,0:T(8,128)S(1)}, f32[512,256]{1,0:T(8,128)S(1)}, u32[]{:S(2)}, u32[]{:S(2)}) %collective-permute-start.19) | collective-permute-done | bytes 524320 | tf_op jit(solution)/shard_map/ppermute | solution.py:127
  172.4 8.1 %fusion.10 = f32[2,2048,256]{2,1,0:T(8,128)} fusion(f32[2,256,256]{2,1,0:T(8,128)S(1)} %fusion.3, f32[2,2048,256]{2,1,0:T(8,128)} %bitcast.97, f32[2,256]{1,0:T(2,128)S(1)} %compare_convert_fusion), kind=kOutput, calls=%fused_computation.12 | convolution fusion | flops 3222274048 | bytes 8914944 | tf_op jit(solution)/shard_map/tnk,tkl->tnl/dot_general | solution.py:131
  180.5 2.6 fusion.21
  186.9 2.3 shard_map.95
  189.2 2.5 shard_map.98
  191.7 6.7 %fusion.1 = f32[2,256,256]{2,1,0:T(8,128)S(1)} fusion(f32[2,2048,256]{2,1,0:T(8,128)S(1)} %bitcast.100, f32[2048,256]{1,0:T(8,128)S(1)} %shard_map.98, f32[2,256]{1,0:T(2,128)S(1)} %compare_convert_fusion), kind=kOutput, calls=%fused_computation.3 | convolution fusion | flops 3222274048 | bytes 6817792 | tf_op jit(solution)/shard_map/nk,tnl->tkl/dot_general | solution.py:131
  198.4 11.6 %collective-permute-done.17 = f32[512,256]{1,0:T(8,128)} collective-permute-done((f32[512,256]{1,0:T(8,128)}, f32[512,256]{1,0:T(8,128)}, u32[]{:S(2)}, u32[]{:S(2)}) %collective-permute-start.17) | collective-permute-done | bytes 524320 | tf_op jit(solution)/shard_map/ppermute | solution.py:127
  211.4 1.8 fusion.26
  213.9 3.9 %subtract_multiply_fusion = f32[2,2048,256]{2,1,0:T(8,128)S(1)} fusion(f32[2,2048,256]{2,1,0:T(8,128)S(1)} %copy-done.19, f32[2,2048,256]{2,1,0:T(8,128)S(1)} %bitcast.86, f32[2,256,256]{2,1,0:T(8,128)S(1)} %fusion.29), kind=kOutput, calls=%fused_computation.2 | convolution fusion | flops 3223322624 | bytes 13107200 | tf_op jit(solution)/shard_map/tnk,tkl->tnl/dot_general | solution.py:131
  217.8 7.0 %convolution_add_fusion.gram_ref = f32[2,256,256]{2,1,0:T(8,128)S(1)} fusion(f32[2,2048,256]{2,1,0:T(8,128)S(1)} %subtract_multiply_fusion, f32[256,256]{1,0:T(8,128)S(1)} %fusion.28, f32[2,256]{1,0:T(2,128)S(1)} %broadcast_subtract_fusion), kind=kOutput, calls=%fused_computation.24 | convolution fusion | flops 3221487616 | bytes 4982784 | tf_op jit(solution)/shard_map/tnk,tnl->tkl/dot_general | solution.py:131
  224.8 13.1 %shard_map.99 = f32[2,256,256]{2,1,0:T(8,128)S(1)} custom-call(f32[2,256,256]{2,1,0:T(8,128)S(1)} %convolution_add_fusion.gram_ref), custom_call_target="tpu_custom_call" | custom-call | tf_op jit(solution)/shard_map/pallas_call | solution.py:115
  237.9 3.8 %convolution_multiply_fusion = f32[2,2048,256]{2,1,0:T(8,128)S(1)} fusion(f32[2,2048,256]{2,1,0:T(8,128)S(1)} %subtract_multiply_fusion, f32[2,256,256]{2,1,0:T(8,128)S(1)} %shard_map.99), kind=kOutput, calls=%fused_computation.14 | convolution fusion | flops 3222274048 | bytes 8912896 | tf_op jit(solution)/shard_map/tnk,tlk->tnl/dot_general | solution.py:131
  241.7 7.5 %fusion.30 = f32[2,256,256]{2,1,0:T(8,128)S(1)} fusion(f32[2,2048,256]{2,1,0:T(8,128)S(1)} %bitcast.87, f32[2,2048,256]{2,1,0:T(8,128)S(1)} %convolution_multiply_fusion), kind=kOutput, calls=%fused_computation.53 | convolution fusion | flops 3221225472 | bytes 8912896 | tf_op jit(solution)/shard_map/tnk,tnl->tkl/dot_general | solution.py:131
  249.2 6.8 %fusion.8 = f32[2,256,256]{2,1,0:T(8,128)S(1)} fusion(f32[2,2048,256]{2,1,0:T(8,128)S(1)} %convolution_multiply_fusion, f32[2,2048,256]{2,1,0:T(8,128)S(1)} %bitcast.98, f32[2,256]{1,0:T(2,128)S(1)} %compare_convert_fusion), kind=kOutput, calls=%fused_computation.10 | convolution fusion | flops 3222274048 | bytes 8914944 | tf_op jit(solution)/shard_map/tnk,tnl->tkl/dot_general | solution.py:131
  257.2 4.0 %fusion.5 = f32[2,2048,256]{2,1,0:T(8,128)S(1)} fusion(f32[2,256,256]{2,1,0:T(8,128)S(1)} %fusion.8, f32[2,2048,256]{2,1,0:T(8,128)S(1)} %bitcast.102, f32[2,256]{1,0:T(2,128)S(1)} %compare_convert_fusion), kind=kOutput, calls=%fused_computation.7 | convolution fusion | flops 3222274048 | bytes 8914944 | tf_op jit(solution)/shard_map/tnk,tkl->tnl/dot_general | solution.py:131
  261.2 5.2 %fusion = f32[2,2048,256]{2,1,0:T(8,128)} fusion(f32[2,2048,256]{2,1,0:T(8,128)S(1)} %fusion.5, f32[2,256,256]{1,2,0:T(8,128)S(1)} %fusion.31, f32[2048,256]{1,0:T(8,128)S(1)} %shard_map.98), kind=kOutput, calls=%fused_computation.1 | convolution fusion | flops 3223322624 | bytes 11010048 | tf_op jit(solution)/shard_map/nk,tkl->tnl/dot_general | solution.py:131
  (96 shorter events, 31.2 us)
Async XLA Ops:
  7.2 32.6 %copy-start.12 = (bf16[64,2048]{1,0:T(8,128)(2,1)S(1)}, bf16[64,2048]{1,0:T(8,128)(2,1)}, u32[]{:S(2)}) copy-start(bf16[64,2048]{1,0:T(8,128)(2,1)} %refs_2_.1) | copy-start | bytes 786436
  7.2 69.5 %copy-start.17 = (s32[2]{0:T(128)S(1)}, s32[2]{0:T(128)}, u32[]{:S(2)}) copy-start(s32[2]{0:T(128)} %refs_1_.3) | copy-start | bytes 28
  7.2 133.8 %all-gather.3.cloned.1.call-start = ((), (), s32[]{:S(2)}) async-start(), calls=%async_computation | async-start | bytes 2621440 | tf_op jit(solution)/shard_map/all_gather | solution.py:252
  7.2 17.0 %collective-permute-start.9 = (f32[512,256]{1,0:T(8,128)}, f32[512,256]{1,0:T(8,128)S(1)}, u32[]{:S(2)}, u32[]{:S(2)}) collective-permute-start(f32[512,256]{1,0:T(8,128)} %refs_6_.1), channel_id=1, source_target_pairs={{0,6},{1,7},{2,4},{3,5},{4,2},{5,3},{6,0},{7,1},{8,14},{9,15},{10,... | collective-permute-start | bytes 1572872 | tf_op jit(solution)/shard_map/ppermute | solution.py:127
  11.2 23.4 %collective-permute-start.8 = (f32[512,256]{1,0:T(8,128)}, f32[512,256]{1,0:T(8,128)S(1)}, u32[]{:S(2)}, u32[]{:S(2)}) collective-permute-start(f32[512,256]{1,0:T(8,128)} %refs_6_.1), channel_id=1, source_target_pairs={{0,4},{1,5},{2,6},{3,7},{4,0},{5,1},{6,2},{7,3},{8,12},{9,13},{10,... | collective-permute-start | bytes 1572872 | tf_op jit(solution)/shard_map/ppermute | solution.py:127
  11.7 23.2 %collective-permute-start.7 = (f32[512,256]{1,0:T(8,128)}, f32[512,256]{1,0:T(8,128)S(1)}, u32[]{:S(2)}, u32[]{:S(2)}) collective-permute-start(f32[512,256]{1,0:T(8,128)} %refs_6_.1), channel_id=1, source_target_pairs={{0,2},{1,3},{2,0},{3,1},{4,6},{5,7},{6,4},{7,5},{8,10},{9,11},{10,... | collective-permute-start | bytes 1572872 | tf_op jit(solution)/shard_map/ppermute | solution.py:127
  34.9 58.0 %copy-start = (f32[512,256]{1,0:T(8,128)S(1)}, f32[512,256]{1,0:T(8,128)}, u32[]{:S(2)}) copy-start(f32[512,256]{1,0:T(8,128)} %refs_1_.2) | copy-start | bytes 1572868
  34.9 69.1 %copy-start.24 = (s32[2,1]{0,1:T(1,128)S(1)}, s32[2,1]{0,1:T(1,128)}, u32[]{:S(2)}) copy-start(s32[2,1]{0,1:T(1,128)} %param.15) | copy-start | bytes 28
  39.8 36.8 %collective-permute-start.10 = (f32[4,512,256]{2,1,0:T(8,128)}, f32[4,512,256]{2,1,0:T(8,128)S(1)}, u32[]{:S(2)}, u32[]{:S(2)}) collective-permute-start(f32[4,512,256]{2,1,0:T(8,128)} %pad_maximum_fusion.1), channel_id=1, source_target_pairs={{0,1},{1,0},{2,3},{3,2},{4,5},{5,4},{6,7},{7,6},{8,9},{9,8},{10,11... | collective-permute-start | bytes 6291464 | tf_op jit(solution)/shard_map/ppermute | solution.py:127
  39.8 27.0 %collective-permute-start.5 = (bf16[64,2048]{1,0:T(8,128)(2,1)S(1)}, bf16[64,2048]{1,0:T(8,128)(2,1)S(1)}, u32[]{:S(2)}, u32[]{:S(2)}) collective-permute-start(bf16[64,2048]{1,0:T(8,128)(2,1)S(1)} %copy-done.12), channel_id=1, source_target_pairs={{0,16},{8,24},{16,0},{24,8},{1,17},{9,25},{17,1},{25,9},{2,18},{10... | collective-permute-start | bytes 786440 | tf_op jit(solution)/shard_map/ppermute | solution.py:127
  42.4 25.1 %collective-permute-start.4 = (bf16[64,2048]{1,0:T(8,128)(2,1)S(1)}, bf16[64,2048]{1,0:T(8,128)(2,1)S(1)}, u32[]{:S(2)}, u32[]{:S(2)}) collective-permute-start(bf16[64,2048]{1,0:T(8,128)(2,1)S(1)} %copy-done.12), channel_id=1, source_target_pairs={{0,8},{8,0},{16,24},{24,16},{1,9},{9,1},{17,25},{25,17},{2,10},{10... | collective-permute-start | bytes 786440 | tf_op jit(solution)/shard_map/ppermute | solution.py:127
  44.0 32.6 %collective-permute-start.6 = (bf16[64,2048]{1,0:T(8,128)(2,1)S(1)}, bf16[64,2048]{1,0:T(8,128)(2,1)}, u32[]{:S(2)}, u32[]{:S(2)}) collective-permute-start(bf16[64,2048]{1,0:T(8,128)(2,1)S(1)} %copy-done.12), channel_id=1, source_target_pairs={{0,24},{8,16},{16,8},{24,0},{1,25},{9,17},{17,9},{25,1},{2,26},{10... | collective-permute-start | bytes 786440 | tf_op jit(solution)/shard_map/ppermute | solution.py:127
  85.7 16.8 %collective-permute-start.13 = (f32[256,512]{1,0:T(8,128)S(1)}, f32[256,512]{1,0:T(8,128)S(1)}, u32[]{:S(2)}, u32[]{:S(2)}) collective-permute-start(f32[256,512]{1,0:T(8,128)S(1)} %shard_map.96.refs_1_), channel_id=1, source_target_pairs={{0,24},{8,16},{16,8},{24,0},{1,25},{9,17},{17,9},{25,1},{2,26},{10... | collective-permute-start | bytes 1572872 | tf_op jit(solution)/shard_map/ppermute | solution.py:127
  86.2 48.9 %collective-permute-start.12 = (f32[256,512]{1,0:T(8,128)S(1)}, f32[256,512]{1,0:T(8,128)}, u32[]{:S(2)}, u32[]{:S(2)}) collective-permute-start(f32[256,512]{1,0:T(8,128)S(1)} %shard_map.96.refs_1_), channel_id=1, source_target_pairs={{0,16},{8,24},{16,0},{24,8},{1,17},{9,25},{17,1},{25,9},{2,18},{10... | collective-permute-start | bytes 1572872 | tf_op jit(solution)/shard_map/ppermute | solution.py:127
  92.8 42.3 %collective-permute-start.11 = (f32[256,512]{1,0:T(8,128)S(1)}, f32[256,512]{1,0:T(8,128)}, u32[]{:S(2)}, u32[]{:S(2)}) collective-permute-start(f32[256,512]{1,0:T(8,128)S(1)} %shard_map.96.refs_1_), channel_id=1, source_target_pairs={{0,8},{8,0},{16,24},{24,16},{1,9},{9,1},{17,25},{25,17},{2,10},{10... | collective-permute-start | bytes 1572872 | tf_op jit(solution)/shard_map/ppermute | solution.py:127
  92.8 51.2 %collective-permute-start.2 = (f32[512,256]{1,0:T(8,128)S(1)}, f32[512,256]{1,0:T(8,128)S(1)}, u32[]{:S(2)}, u32[]{:S(2)}) collective-permute-start(f32[512,256]{1,0:T(8,128)S(1)} %copy-done), channel_id=1, source_target_pairs={{0,6},{1,7},{2,4},{3,5},{4,2},{5,3},{6,0},{7,1},{8,14},{9,15},{10,... | collective-permute-start | bytes 1572872 | tf_op jit(solution)/shard_map/ppermute | solution.py:127
  95.2 48.8 %collective-permute-start.1 = (f32[512,256]{1,0:T(8,128)S(1)}, f32[512,256]{1,0:T(8,128)S(1)}, u32[]{:S(2)}, u32[]{:S(2)}) collective-permute-start(f32[512,256]{1,0:T(8,128)S(1)} %copy-done), channel_id=1, source_target_pairs={{0,4},{1,5},{2,6},{3,7},{4,0},{5,1},{6,2},{7,3},{8,12},{9,13},{10,... | collective-permute-start | bytes 1572872 | tf_op jit(solution)/shard_map/ppermute | solution.py:127
  102.5 41.6 %collective-permute-start = (f32[512,256]{1,0:T(8,128)S(1)}, f32[512,256]{1,0:T(8,128)S(1)}, u32[]{:S(2)}, u32[]{:S(2)}) collective-permute-start(f32[512,256]{1,0:T(8,128)S(1)} %copy-done), channel_id=1, source_target_pairs={{0,2},{1,3},{2,0},{3,1},{4,6},{5,7},{6,4},{7,5},{8,10},{9,11},{10,... | collective-permute-start | bytes 1572872 | tf_op jit(solution)/shard_map/ppermute | solution.py:127
  140.9 39.6 %collective-permute-start.14 = (f32[4,512,256]{2,1,0:T(8,128)}, f32[4,512,256]{2,1,0:T(8,128)}, u32[]{:S(2)}, u32[]{:S(2)}) collective-permute-start(f32[4,512,256]{2,1,0:T(8,128)} %get-tuple-element.5), channel_id=1, source_target_pairs={{0,1},{1,0},{2,3},{3,2},{4,5},{5,4},{6,7},{7,6},{8,9},{9,8},{10,11... | collective-permute-start | bytes 6291464 | tf_op jit(solution)/shard_map/ppermute | solution.py:127
  142.6 14.4 %collective-permute-start.18 = (f32[512,256]{1,0:T(8,128)S(1)}, f32[512,256]{1,0:T(8,128)S(1)}, u32[]{:S(2)}, u32[]{:S(2)}) collective-permute-start(f32[512,256]{1,0:T(8,128)S(1)} %get-tuple-element.13), channel_id=1, source_target_pairs={{0,4},{1,5},{2,6},{3,7},{4,0},{5,1},{6,2},{7,3},{8,12},{9,13},{10,... | collective-permute-start | bytes 1572872 | tf_op jit(solution)/shard_map/ppermute | solution.py:127
  144.1 12.8 %copy-start.4 = (f32[512,256]{1,0:T(8,128)}, f32[512,256]{1,0:T(8,128)S(1)}, u32[]{:S(2)}) copy-start(f32[512,256]{1,0:T(8,128)S(1)} %collective-permute-done.refs_2_) | copy-start | bytes 1572868
  145.6 41.3 %collective-permute-start.3 = (f32[4,512,256]{2,1,0:T(8,128)}, f32[4,512,256]{2,1,0:T(8,128)}, u32[]{:S(2)}, u32[]{:S(2)}) collective-permute-start(f32[4,512,256]{2,1,0:T(8,128)} %pad_maximum_fusion), channel_id=1, source_target_pairs={{0,1},{1,0},{2,3},{3,2},{4,5},{5,4},{6,7},{7,6},{8,9},{9,8},{10,11... | collective-permute-start | bytes 6291464 | tf_op jit(solution)/shard_map/ppermute | solution.py:127
  145.8 14.7 %collective-permute-start.20 = (f32[512,256]{1,0:T(8,128)S(1)}, f32[512,256]{1,0:T(8,128)S(1)}, u32[]{:S(2)}, u32[]{:S(2)}) collective-permute-start(f32[512,256]{1,0:T(8,128)S(1)} %get-tuple-element.11), channel_id=1, source_target_pairs={{0,2},{1,3},{2,0},{3,1},{4,6},{5,7},{6,4},{7,5},{8,10},{9,11},{10,... | collective-permute-start | bytes 1572872 | tf_op jit(solution)/shard_map/ppermute | solution.py:127
  147.3 23.9 %collective-permute-start.19 = (f32[512,256]{1,0:T(8,128)S(1)}, f32[512,256]{1,0:T(8,128)S(1)}, u32[]{:S(2)}, u32[]{:S(2)}) collective-permute-start(f32[512,256]{1,0:T(8,128)S(1)} %get-tuple-element.12), channel_id=1, source_target_pairs={{0,6},{1,7},{2,4},{3,5},{4,2},{5,3},{6,0},{7,1},{8,14},{9,15},{10,... | collective-permute-start | bytes 1572872 | tf_op jit(solution)/shard_map/ppermute | solution.py:127
  172.3 16.9 %collective-permute-start.21 = (f32[2,512,256]{2,1,0:T(8,128)}, f32[2,512,256]{2,1,0:T(8,128)}, u32[]{:S(2)}, u32[]{:S(2)}) collective-permute-start(f32[2,512,256]{2,1,0:T(8,128)} %pad_maximum_fusion.2), channel_id=1, source_target_pairs={{0,1},{1,0},{2,3},{3,2},{4,5},{5,4},{6,7},{7,6},{8,9},{9,8},{10,11... | collective-permute-start | bytes 3145736 | tf_op jit(solution)/shard_map/ppermute | solution.py:127
  172.4 8.2 %copy-start.2 = (f32[4,512,256]{2,1,0:T(8,128)S(1)}, f32[4,512,256]{2,1,0:T(8,128)}, u32[]{:S(2)}) copy-start(f32[4,512,256]{2,1,0:T(8,128)} %copy-done.1) | copy-start | bytes 6291460
  183.2 15.2 %collective-permute-start.15 = (f32[512,256]{1,0:T(8,128)}, f32[512,256]{1,0:T(8,128)}, u32[]{:S(2)}, u32[]{:S(2)}) collective-permute-start(f32[512,256]{1,0:T(8,128)} %get-tuple-element.6), channel_id=1, source_target_pairs={{0,2},{1,3},{2,0},{3,1},{4,6},{5,7},{6,4},{7,5},{8,10},{9,11},{10,... | collective-permute-start | bytes 1572872 | tf_op jit(solution)/shard_map/ppermute | solution.py:127
  184.6 25.4 %collective-permute-start.17 = (f32[512,256]{1,0:T(8,128)}, f32[512,256]{1,0:T(8,128)}, u32[]{:S(2)}, u32[]{:S(2)}) collective-permute-start(f32[512,256]{1,0:T(8,128)} %get-tuple-element.7), channel_id=1, source_target_pairs={{0,6},{1,7},{2,4},{3,5},{4,2},{5,3},{6,0},{7,1},{8,14},{9,15},{10,... | collective-permute-start | bytes 1572872 | tf_op jit(solution)/shard_map/ppermute | solution.py:127
  186.1 25.3 %collective-permute-start.16 = (f32[512,256]{1,0:T(8,128)}, f32[512,256]{1,0:T(8,128)}, u32[]{:S(2)}, u32[]{:S(2)}) collective-permute-start(f32[512,256]{1,0:T(8,128)} %get-tuple-element.8), channel_id=1, source_target_pairs={{0,4},{1,5},{2,6},{3,7},{4,0},{5,1},{6,2},{7,3},{8,12},{9,13},{10,... | collective-permute-start | bytes 1572872 | tf_op jit(solution)/shard_map/ppermute | solution.py:127
  191.7 22.2 %copy-start.19 = (f32[2,2048,256]{2,1,0:T(8,128)S(1)}, f32[2,2048,256]{2,1,0:T(8,128)}, u32[]{:S(2)}) copy-start(f32[2,2048,256]{2,1,0:T(8,128)} %fusion.10) | copy-start | bytes 12582916
  241.7 7.5 %copy-start.18 = (f32[2,2048,256]{2,1,0:T(8,128)}, f32[2,2048,256]{2,1,0:T(8,128)S(1)}, u32[]{:S(2)}) copy-start(f32[2,2048,256]{2,1,0:T(8,128)S(1)} %convolution_multiply_fusion) | copy-start | bytes 12582916
  249.2 7.9 %copy-start.23 = (f32[4096,256]{1,0:T(8,128)S(1)}, f32[4096,256]{1,0:T(8,128)}, u32[]{:S(2)}) copy-start(f32[4096,256]{1,0:T(8,128)} %param.13) | copy-start | bytes 12582916
  (16 other events, 34.5 us)
Sparse Core Ops, SparseCore 0:
  12.0 66.7 all-gather.2
where the time goes:
time: 278 us; the launch traced here: 273 us
  waiting for transfers between devices  118 us (42%)
  matrix products  63.8 us (23%)
  starting transfers between devices  27.9 us (10%)
  Pallas kernels  25.3 us (9%)
  between operations  14.5 us (5%)
  local copies, waits for them, and re-layouts  13 us (5%)
  other arithmetic  11.1 us (4%)
    ppermute x22, waiting for transfers between devices, flip(): return lax.ppermute(value, axis, [(i, i ^ mask) for i in range(size)])  118 us
    dot_general x12, matrix products, dot(): jnp.einsum(spec, a, b, precision=highest, preferred_element_type=jnp.floa...  63.8 us
    ppermute x22, starting transfers between devices, flip(): return lax.ppermute(value, axis, [(i, i ^ mask) for i in range(size)])  27.8 us
    pallas_call x1, Pallas kernels, factor(): pl.pallas_call(factor_kernel, out_shape=jax.ShapeDtypeStruct(gram.shape,...  13.1 us
    pallas_call x4, Pallas kernels, call(): pl.pallas_call(kernel, out_shape=shapes, in_specs=[pl.BlockSpec(memory_sp...  12.2 us
    unnamed x50, local copies, waits for them, and re-layouts  11.3 us
  transfers between devices with their start and end apart: 23, of which 12 were waited for; matrix products, arithmetic and copies ran while one was open for 13% of the time, Pallas kernels for 4%

commit v1 on v0

--- a/solution.py
+++ b/solution.py
@@ -127,104 +127,171 @@
     return lax.ppermute(value, axis, [(i, i ^ mask) for i in range(size)])
 
 
+def after(value, *earlier):
+    return lax.optimization_barrier((value, *earlier))[0]
+
+
 def dot(spec, a, b):
     return jnp.einsum(spec, a, b, precision=highest, preferred_element_type=jnp.float32)
 
 
-def call(kernel, out, args, kinds, scratch=(), limit=40):
+def shaped(shape, dtype=jnp.float32):
+    return jax.ShapeDtypeStruct(shape, dtype)
+
+
+def call(kernel, out, args, kinds, scratch=(), limit=48, flops=0):
     spaces = {"v": pltpu.VMEM, "s": pltpu.SMEM, "a": pl.ANY}
-    flat = jax.tree.leaves(out)
-    shapes = [jax.ShapeDtypeStruct(s.shape, s.dtype) for s in flat]
-    where = pl.ANY if kinds[-1] == "a" else pltpu.VMEM
-    result = pl.pallas_call(
+    moved = sum(a.size * a.dtype.itemsize for a in [*out, *args])
+    return pl.pallas_call(
         kernel,
-        out_shape=shapes,
-        in_specs=[pl.BlockSpec(memory_space=spaces[k]) for k in kinds[:-1]],
-        out_specs=[pl.BlockSpec(memory_space=where)] * len(shapes),
+        out_shape=out,
+        in_specs=[pl.BlockSpec(memory_space=spaces[k]) for k in kinds[: len(args)]],
+        out_specs=[pl.BlockSpec(memory_space=spaces[k]) for k in kinds[len(args) :]],
         scratch_shapes=list(scratch),
         compiler_params=pltpu.CompilerParams(vmem_limit_bytes=limit * 1024 * 1024),
+        cost_estimate=pl.CostEstimate(flops=flops, bytes_accessed=moved, transcendentals=0),
     )(*args)
-    return result
-
-
-def shaped(shape, dtype=jnp.float32):
-    return jax.ShapeDtypeStruct(shape, dtype)
+
+
+def power_of_two(exponent):
+    low = exponent + 128
+    value = jnp.full(exponent.shape, 2.0**-64, jnp.float32)
+    for bit in range(7):
+        value = value * jnp.where((low >> bit) & 1 == 1, 2.0 ** (2**bit), 1.0)
+    return value * jnp.where(low >= 128, 1.0, 2.0**-64) * jnp.where(low >= 128, 2.0**64, 1.0)
+
+
+def packed_rows(rows):
+    return rows // 4 * 3 + 8
+
+
+def pack_into(value, out_ref):
+    rows, width = value.shape
+    piece = rows // 4
+    top = jnp.max(jnp.abs(value), axis=0, keepdims=True)
+    level = jnp.log(jnp.maximum(top, 2.0**-90)) * 1.4426950408889634
+    exponent = jnp.floor(level).astype(jnp.int32) + 1
+    factor_up = power_of_two(23 - exponent)
+    limit = 2.0**23 - 1
+    codes = [
+        jnp.clip(jnp.round(value[piece * n : piece * (n + 1)] * factor_up), -limit, limit).astype(jnp.int32)
+        for n in range(4)
+    ]
+    for n in range(3):
+        out_ref[piece * n : piece * (n + 1), :] = (codes[n] << 8) | ((codes[3] >> (8 * n)) & 255)
+    out_ref[3 * piece :, :] = jnp.broadcast_to(exponent, (8, width))
+
+
+def unpack(words):
+    rows, width = words.shape
+    piece = (rows - 8) // 3
+    part = [words[piece * n : piece * (n + 1)] for n in range(3)]
+    down = power_of_two(words[3 * piece : 3 * piece + 1] - 23)
+    last = ((part[2] << 24) | ((part[1] & 255) << 16) | ((part[0] & 255) << 8)) >> 8
+    codes = [p >> 8 for p in part] + [last]
+    return [c.astype(jnp.float32) * down for c in codes]
+
+
+def load_all(pairs_of, sem):
+    copies = [pltpu.make_async_copy(src, dst, sem.at[n]) for n, (src, dst) in enumerate(pairs_of)]
+    for c in copies:
+        c.start()
+    for c in copies:
+        c.wait()
+
+
+def pack_kernel(value_ref, out_ref):
+    pack_into(value_ref[...], out_ref)
 
 
 def solve_kernel(rows, pairs, where_ref, rank_ref, *refs):
     inverse, held, other = refs[:rows], refs[rows : rows + pairs], refs[rows + pairs]
-    out_ref, whole = refs[rows + pairs + 1 :]
+    out_ref, packed_ref, whole, right, sem = refs[rows + pairs + 1 :]
     floor, me = where_ref[0], where_ref[1]
     part = inverse[0].shape[0]
     chunk, cap = held[0].shape
     quarters = pairs
     half, quarter = me // quarters, me % quarters
-    for d in range(rows):
-        whole[pl.ds(pl.multiple_of((floor ^ d) * part, part), part), :] = inverse[d][...]
+    moves = [
+        (inverse[d], whole.at[pl.ds(pl.multiple_of((floor ^ d) * part, part), part), :]) for d in range(rows)
+    ]
+    for at in range(2 * pairs):
+        moves.append((held[at // 2] if at % 2 == 0 else other.at[at // 2], right.at[at]))
+    load_all(moves, sem)
     column = lax.broadcasted_iota(jnp.int32, (1, cap), 1)
     for h in range(2):
         total = None
         for d in range(quarters):
-            at = h * quarters + d
-            value = held[at // 2][...] if at % 2 == 0 else other[at // 2]
             lhs = whole[:, pl.ds(pl.multiple_of((quarter ^ d) * chunk, chunk), chunk)]
-            for piece in split_three(value):
+            for piece in split_three(right[h * quarters + d]):
                 term = jnp.dot(lhs, piece, preferred_element_type=jnp.float32)
                 total = term if total is None else total + term
         tile = half ^ h
         kept = column < rank_ref[tile]
         out_ref[:, pl.ds(pl.multiple_of(tile * cap, cap), cap)] = jnp.where(kept, total, 0.0)
-
-
-def core_kernel(rows, pairs, where_ref, *refs):
-    solved, (mine_ref, theirs_ref) = refs[:rows], refs[rows:]
+    pack_into(out_ref[...], packed_ref)
+
+
+def core_kernel(rows, pairs, where_ref, own_ref, *refs):
+    arrived, (mine_ref, theirs_ref, solved, sem) = refs[: rows - 1], refs[rows - 1 :]
     floor, me = where_ref[0], where_ref[1]
     pair, side = me // 2, me % 2
     cap = mine_ref.shape[2]
-    own = solved[0][...]
-    own_high = own.astype(jnp.bfloat16)
-    own_low = (own - own_high.astype(jnp.float32)).astype(jnp.bfloat16)
+    own = own_ref[...]
+    load_all([(arrived[d], solved.at[d]) for d in range(rows - 1)], sem)
+
+    def halves(x):
+        high = x.astype(jnp.bfloat16)
+        return high, (x - high.astype(jnp.float32)).astype(jnp.bfloat16)
+
+    own_high, own_low = halves(own)
 
     def across(x, y):
         return lax.dot_general(x, y, (((0,), (0,)), ((), ())), preferred_element_type=jnp.float32)
 
     for e in range(pairs):
         wanted = floor ^ pair ^ e
-        value = own
-        for d in range(1, rows):
-            value = jnp.where(wanted == d, solved[d][...], value)
-        high = value.astype(jnp.bfloat16)
-        low = (value - high.astype(jnp.float32)).astype(jnp.bfloat16)
+        there = jnp.concatenate(unpack(solved[jnp.maximum(wanted, 1) - 1]), axis=0)
+        high, low = halves(jnp.where(wanted == 0, own, there))
         part = across(own_high, high) + (across(own_high, low) + across(own_low, high))
         left, right = part[:, :cap], part[:, cap:]
         mine_ref[e] = jnp.where(side == 0, left, right)
         theirs_ref[e] = jnp.where(side == 0, right, left)
 
 
-def place_kernel(count, slot_ref, *refs):
-    blocks, out_ref, sem = refs[: -2], refs[-2], refs[-1]
+def choose_kernel(rows, pairs, where_ref, *refs):
+    ins, outs, sem = refs[:rows], refs[rows : rows + pairs], refs[rows + pairs]
+    mark = where_ref[0] ^ (where_ref[1] // 2)
+    for g in range(rows):
+
+        @pl.when(mark == g)
+        def _(g=g):
+            load_all([(ins[g ^ e], outs[e]) for e in range(pairs)], sem)
+
+
+def spread_kernel(count, slot_ref, *refs):
+    blocks, (out_ref, words, sem) = refs[:-3], refs[-3:]
     flat = []
     for b in blocks:
         flat += [b] if len(b.shape) == 2 else [b.at[i] for i in range(b.shape[0])]
-    copies = []
+    load_all([(flat[n], words.at[n]) for n in range(count)], sem)
     for n in range(count):
-        chunk = flat[n].shape[0]
-        at = pl.multiple_of(slot_ref[n] * chunk, chunk)
-        copies.append(pltpu.make_async_copy(flat[n], out_ref.at[pl.ds(at, chunk)], sem.at[n]))
-    for c in copies:
-        c.start()
-    for c in copies:
-        c.wait()
-
-
-def place(slots, blocks, count):
-    chunk, width = blocks[0].shape[-2:]
+        values = unpack(words[n])
+        piece = values[0].shape[0]
+        for i in range(4):
+            at = pl.multiple_of(slot_ref[n] * (4 * piece) + piece * i, piece)
+            out_ref[pl.ds(at, piece), :] = values[i]
+
+
+def spread(slots, blocks, count):
+    words, width = blocks[0].shape[-2:]
+    chunk = (words - 8) // 3 * 4
     return call(
-        lambda *refs: place_kernel(count, *refs),
+        lambda *refs: spread_kernel(count, *refs),
         [shaped((count * chunk, width))],
         [jnp.stack(slots), *blocks],
-        "s" + "a" * (len(blocks) + 1),
-        [pltpu.SemaphoreType.DMA((count,))],
+        "s" + "a" * len(blocks) + "v",
+        [pltpu.VMEM((count, words, width), jnp.int32), pltpu.SemaphoreType.DMA((count,))],
     )[0]
 
 
@@ -243,28 +310,46 @@
         spot = jnp.stack([floor, me])
         columns = jnp.arange(rank_cap, dtype=jnp.int32)
         my_pair, my_side = me // 2, me % 2
-
-        def row_gather(block):
-            held = [block] + [flip(block, "col", cols, 2 * d) for d in range(1, pairs)]
-            return held, flip(jnp.stack(held), "col", cols, 1)
+        wide = tile_rows * rank_cap
 
         inverse = [factor_inverse] + [flip(factor_inverse, "row", rows, d) for d in range(1, rows)]
-        slices = lax.all_gather(panel_left, "row", axis=0)
-        held, other = row_gather(panel_right)
-        solved = call(
+        held = [panel_right] + [flip(panel_right, "col", cols, 2 * d) for d in range(1, pairs)]
+        other = flip(jnp.stack(held), "col", cols, 1)
+
+        words = call(pack_kernel, [shaped((packed_rows(chunk), rank_cap), jnp.int32)], [panel_left], "vv")[0]
+        words_z = after(words, *inverse[1:])
+        from_floors = [words_z] + [flip(words_z, "row", rows, d) for d in range(1, rows)]
+        words_p = after(words, *held[1:])
+        row_held = [words_p] + [flip(words_p, "col", cols, 2 * d) for d in range(1, pairs)]
+
+        solved, solved_words = call(
             lambda *refs: solve_kernel(rows, pairs, *refs),
-            [shaped((rows * part, tile_rows * rank_cap))],
+            [shaped((rows * part, wide)), shaped((packed_rows(rows * part), wide), jnp.int32)],
             [spot, panel_rank, *inverse, *held, other],
-            "ss" + "v" * (rows + pairs + 2),
-            [pltpu.VMEM((rows * part, tile_order), jnp.bfloat16)],
-        )[0]
-        all_solved = [solved] + [flip(solved, "row", rows, d) for d in range(1, rows)]
-
-        held, other = row_gather(panel_left)
-        row_left = place([me ^ (2 * d) for d in range(pairs)] + [me ^ (2 * d + 1) for d in range(pairs)], [*held, other], cols)
-        row_left = row_left.reshape(tile_rows, tile_order, rank_cap)
-
-        got = [lax.dynamic_index_in_dim(slices, my_pair ^ d, 0, keepdims=False) for d in range(pairs)]
+            "ss" + "a" * (rows + pairs + 1) + "vv",
+            [
+                pltpu.VMEM((rows * part, tile_order), jnp.bfloat16),
+                pltpu.VMEM((cols, chunk, rank_cap), jnp.float32),
+                pltpu.SemaphoreType.DMA((rows + cols,)),
+            ],
+            flops=6 * rows * part * tile_order * wide,
+        )
+        arrived = [flip(solved_words, "row", rows, d) for d in range(1, rows)]
+
+        row_other = flip(jnp.stack(row_held), "col", cols, 1)
+        row_left = spread(
+            [me ^ (2 * d) for d in range(pairs)] + [me ^ (2 * d + 1) for d in range(pairs)],
+            [*row_held, row_other],
+            cols,
+        ).reshape(tile_rows, tile_order, rank_cap)
+
+        got = call(
+            lambda *refs: choose_kernel(rows, pairs, *refs),
+            [shaped(words.shape, jnp.int32)] * pairs,
+            [spot, *from_floors],
+            "s" + "a" * (rows + pairs),
+            [pltpu.SemaphoreType.DMA((pairs,))],
+        )
         got = [flip(got[d], "col", cols, 2 * d) if d else got[d] for d in range(pairs)]
         half = pairs // 2
         top = my_pair // half
@@ -273,7 +358,7 @@
         give = [jnp.where(upper, got[d], got[half + d]) for d in range(half)]
         take = flip(jnp.stack(give), "col", cols, 1)
         low = my_pair % half
-        col_left = place(
+        col_left = spread(
             [2 * (low ^ d) + my_side for d in range(half)] + [2 * (low ^ d) + 1 - my_side for d in range(half)],
             [*keep, take],
             pairs,
@@ -281,9 +366,14 @@
 
         mine, theirs = call(
             lambda *refs: core_kernel(rows, pairs, *refs),
-            [shaped((pairs, tile_rows * rank_cap, rank_cap))] * 2,
-            [spot, *all_solved],
-            "s" + "v" * (rows + 1),
+            [shaped((pairs, wide, rank_cap))] * 2,
+            [spot, solved, *arrived],
+            "sv" + "a" * (rows - 1) + "vv",
+            [
+                pltpu.VMEM((rows - 1, *solved_words.shape), jnp.int32),
+                pltpu.SemaphoreType.DMA((rows - 1,)),
+            ],
+            flops=6 * rows * part * wide * wide * pairs,
         )
         theirs = flip(theirs, "col", cols, 1)
         parts = [mine[e] + theirs[e] for e in range(pairs)]

time: 278 us -> 264 us (0.950)
  waiting for transfers between devices: 118 us -> 93.9 us
  starting transfers between devices: 27.9 us -> 49.2 us
  between operations: 14.5 us -> 1.52 us
  Pallas kernels: 25.3 us -> 33.3 us
  local copies, waits for them, and re-layouts: 13 us -> 6.52 us
    ppermute x22 -> x25, waiting for transfers between devices: 118 us -> 93.9 us  [flip(): return lax.ppermute(value, axis, [(i, i ^ mask) for i in range(size)])]
    ppermute x22 -> x25, starting transfers between devices: 27.8 us -> 49.2 us  [flip(): return lax.ppermute(value, axis, [(i, i ^ mask) for i in range(size)])]
    pallas_call x4 -> x6, Pallas kernels: 12.2 us -> 20.4 us  [call(): pl.pallas_call(kernel, out_shape=out, in_specs=[pl.BlockSpec(memory_space...]
    unnamed x50 -> x54, local copies, waits for them, and re-layouts: 11.3 us -> 6.44 us
  transfers between devices with their start and end apart: 23 -> 25, of which waited for: 12 -> 13; matrix products, arithmetic and copies ran while one was open for 13% -> 11% of each run, Pallas kernels for 4% -> 6%
where the time goes in v1:
time: 264 us; the launch traced here: 259 us
  waiting for transfers between devices  93.9 us (36%)
  matrix products  64.2 us (24%)
  starting transfers between devices  49.2 us (19%)
  Pallas kernels  33.3 us (13%)
  other arithmetic  10.4 us (4%)
  local copies, waits for them, and re-layouts  6.52 us (2%)
    ppermute x25, waiting for transfers between devices, flip(): return lax.ppermute(value, axis, [(i, i ^ mask) for i in range(size)])  93.9 us
    dot_general x12, matrix products, dot(): jnp.einsum(spec, a, b, precision=highest, preferred_element_type=jnp.floa...  64.2 us
    ppermute x25, starting transfers between devices, flip(): return lax.ppermute(value, axis, [(i, i ^ mask) for i in range(size)])  49.2 us
    pallas_call x6, Pallas kernels, call(): pl.pallas_call(kernel, out_shape=out, in_specs=[pl.BlockSpec(memory_space...  20.4 us
    pallas_call x1, Pallas kernels, factor(): pl.pallas_call(factor_kernel, out_shape=jax.ShapeDtypeStruct(gram.shape,...  12.9 us
    unnamed x54, local copies, waits for them, and re-layouts  6.44 us
  transfers between devices with their start and end apart: 25, of which 13 were waited for; matrix products, arithmetic and copies ran while one was open for 11% of the time, Pallas kernels for 6%

profile of v1, /device:TPU:0, one launch (start us, length us, event | category | flops | bytes accessed | tf_op | source)
XLA Modules:
  0.0 259.0 jit_solution(15096738076206243661)
XLA Ops:
  0.7 4.0 %collective-permute-start.2 = (f32[512,256]{1,0:T(8,128)}, f32[512,256]{1,0:T(8,128)S(1)}, u32[]{:S(2)}, u32[]{:S(2)}) collective-permute-start(f32[512,256]{1,0:T(8,128)} %refs_6_.1), channel_id=1, source_target_pairs={{0,6},{1,7},{2,4},{3,5},{4,2},{5,3},{6,0},{7,1},{8,14},{9,15},{10,... | collective-permute-start | bytes 1572872 | tf_op jit(solution)/shard_map/ppermute | solution.py:127
  5.3 12.4 %collective-permute-done.2.refs_9_ = f32[512,256]{1,0:T(8,128)S(1)} collective-permute-done((f32[512,256]{1,0:T(8,128)}, f32[512,256]{1,0:T(8,128)S(1)}, u32[]{:S(2)}, u32[]{:S(2)}) %collective-permute-start.2) | collective-permute-done | bytes 524320 | tf_op jit(solution)/shard_map/ppermute | solution.py:127
  17.6 10.4 %collective-permute-done.1.refs_8_ = f32[512,256]{1,0:T(8,128)S(1)} collective-permute-done((f32[512,256]{1,0:T(8,128)}, f32[512,256]{1,0:T(8,128)S(1)}, u32[]{:S(2)}, u32[]{:S(2)}) %collective-permute-start.1) | collective-permute-done | bytes 524320 | tf_op jit(solution)/shard_map/ppermute | solution.py:127
  28.3 2.6 %pad_maximum_fusion = f32[4,512,256]{2,1,0:T(8,128)} fusion(f32[1,512,256]{2,1,0:T(8,128)S(1)} %bitcast.79, f32[1,512,256]{2,1,0:T(8,128)S(1)} %bitcast.80, f32[1,512,256]{2,1,0:T(8,128)S(1)} %bitcast.81, f32[1,512,256]{2,1,0:T(8,128)} %bitcast.78), kind=kLoop, calls=%fused_computation.15 | loop fusion | flops 1572864 | bytes 4194304 | tf_op jit(solution)/shard_map/stack | solution.py:317
  30.9 2.6 collective-permute-start.8
  35.4 11.2 %collective-permute-done.8.refs_4_ = bf16[64,2048]{1,0:T(8,128)(2,1)S(1)} collective-permute-done((bf16[64,2048]{1,0:T(8,128)(2,1)S(1)}, bf16[64,2048]{1,0:T(8,128)(2,1)S(1)}, u32[]{:S(2)}, u32[]{:S(2)}) %collective-permute-start.8) | collective-permute-done | bytes 262176 | tf_op jit(solution)/shard_map/ppermute | solution.py:127
  46.6 6.5 %collective-permute-done.9.refs_5_ = bf16[64,2048]{1,0:T(8,128)(2,1)} collective-permute-done((bf16[64,2048]{1,0:T(8,128)(2,1)S(1)}, bf16[64,2048]{1,0:T(8,128)(2,1)}, u32[]{:S(2)}, u32[]{:S(2)}) %collective-permute-start.9) | collective-permute-done | bytes 262176 | tf_op jit(solution)/shard_map/ppermute | solution.py:127
  53.0 5.2 %shard_map.97 = (f32[256,512]{1,0:T(8,128)S(1)}, s32[200,512]{1,0:T(8,128)}) custom-call(s32[2]{0:T(128)S(1)} %pad_add_fusion.2.refs_0_, s32[2]{0:T(128)S(1)} %copy-done.15, bf16[64,2048]{1,0:T(8,128)(2,1)S(1)} %copy-done.14, bf16[64,2048]{1,0:T(8,128)(2,1)} %collective-permute-done.7.refs_3_, bf16[64,2048]{1,0:T(8,128)(2,1)S(1)} %collective-permute-done.8.refs_4_, ...), custom_call_target="tpu_custom_call" | custom-call | flops 1610612736 | bytes 6176784 | tf_op jit(solution)/shard_map/pallas_call | solution.py:145
  58.3 2.5 collective-permute-start.13
  60.8 4.6 %collective-permute-start.12 = (s32[200,512]{1,0:T(8,128)}, s32[200,512]{1,0:T(8,128)S(1)}, u32[]{:S(2)}, u32[]{:S(2)}) collective-permute-start(s32[200,512]{1,0:T(8,128)} %get-tuple-element.14), channel_id=1, source_target_pairs={{0,16},{8,24},{16,0},{24,8},{1,17},{9,25},{17,1},{25,9},{2,18},{10... | collective-permute-start | bytes 1228808 | tf_op jit(solution)/shard_map/ppermute | solution.py:127
  66.1 2.4 collective-permute-start.20
  69.2 3.7 %collective-permute-done.13.refs_4_ = s32[200,512]{1,0:T(8,128)S(1)} collective-permute-done((s32[200,512]{1,0:T(8,128)}, s32[200,512]{1,0:T(8,128)S(1)}, u32[]{:S(2)}, u32[]{:S(2)}) %collective-permute-start.13) | collective-permute-done | bytes 409632 | tf_op jit(solution)/shard_map/ppermute | solution.py:127
  73.7 18.0 %collective-permute-start.18 = (s32[392,256]{1,0:T(8,128)S(1)}, s32[392,256]{1,0:T(8,128)}, u32[]{:S(2)}, u32[]{:S(2)}) collective-permute-start(s32[392,256]{1,0:T(8,128)S(1)} %shard_map.95.refs_1_), channel_id=1, source_target_pairs={{0,8},{8,0},{16,24},{24,16},{1,9},{9,1},{17,25},{25,17},{2,10},{10... | collective-permute-start | bytes 1204232 | tf_op jit(solution)/shard_map/ppermute | solution.py:127
  91.6 23.4 %collective-permute-done.12.refs_3_ = s32[200,512]{1,0:T(8,128)S(1)} collective-permute-done((s32[200,512]{1,0:T(8,128)}, s32[200,512]{1,0:T(8,128)S(1)}, u32[]{:S(2)}, u32[]{:S(2)}) %collective-permute-start.12) | collective-permute-done | bytes 409632 | tf_op jit(solution)/shard_map/ppermute | solution.py:127
  120.6 4.5 %shard_map.98 = (f32[4,512,256]{2,1,0:T(8,128)S(1)}, f32[4,512,256]{2,1,0:T(8,128)}) custom-call(s32[2]{0:T(128)S(1)} %pad_add_fusion.2.refs_0_, f32[256,512]{1,0:T(8,128)S(1)} %copy-done.17, s32[200,512]{1,0:T(8,128)S(1)} %copy-done.13, s32[200,512]{1,0:T(8,128)S(1)} %copy-done.11, s32[200,512]{1,0:T(8,128)S(1)} %copy-done.9), custom_call_target="tpu_custom_call" | custom-call | flops 1610612736 | bytes 5947400 | tf_op jit(solution)/shard_map/pallas_call | solution.py:145
  128.3 3.9 %collective-permute-done.19.refs_3_ = s32[392,256]{1,0:T(8,128)S(1)} collective-permute-done((s32[392,256]{1,0:T(8,128)S(1)}, s32[392,256]{1,0:T(8,128)S(1)}, u32[]{:S(2)}, u32[]{:S(2)}) %collective-permute-start.19) | collective-permute-done | bytes 401440 | tf_op jit(solution)/shard_map/ppermute | solution.py:127
  136.9 8.6 %fusion.3 = f32[2,256,256]{2,1,0:T(8,128)S(1)} fusion(f32[2,2048,256]{2,1,0:T(8,128)S(1)} %bitcast.88, f32[2,2048,256]{2,1,0:T(8,128)} %bitcast.89, f32[2,256]{1,0:T(2,128)S(1)} %compare_convert_fusion), kind=kOutput, calls=%fused_computation.5 | convolution fusion | flops 3223322624 | bytes 8914944 | tf_op jit(solution)/shard_map/tnk,tnl->tkl/dot_general | solution.py:135
  149.4 14.3 %collective-permute-done.21 = s32[392,256]{1,0:T(8,128)S(1)} collective-permute-done((s32[392,256]{1,0:T(8,128)S(1)}, s32[392,256]{1,0:T(8,128)S(1)}, u32[]{:S(2)}, u32[]{:S(2)}) %collective-permute-start.21) | collective-permute-done | bytes 401440 | tf_op jit(solution)/shard_map/ppermute | solution.py:127
  166.3 4.9 %fusion.10 = f32[2,2048,256]{2,1,0:T(8,128)} fusion(f32[2,256,256]{2,1,0:T(8,128)S(1)} %fusion.3, f32[2,2048,256]{2,1,0:T(8,128)S(1)} %bitcast.85, f32[2,256]{1,0:T(2,128)S(1)} %compare_convert_fusion), kind=kOutput, calls=%fused_computation.12 | convolution fusion | flops 3222274048 | bytes 8914944 | tf_op jit(solution)/shard_map/tnk,tkl->tnl/dot_general | solution.py:135
  171.3 2.7 %fusion.21 = (f32[512,256]{1,0:T(8,128)}, f32[512,256]{1,0:T(8,128)}, f32[512,256]{1,0:T(8,128)}) fusion(f32[4,512,256]{2,1,0:T(8,128)} %collective-permute-done.14, f32[4,512,256]{2,1,0:T(8,128)S(1)} %get-tuple-element.15), kind=kLoop, calls=%fused_computation.31 | loop fusion | flops 393216 | bytes 4718592 | tf_op jit(solution)/shard_map/add | solution.py:379
  178.4 2.5 shard_map.100
  180.9 8.7 %fusion.1 = f32[2,256,256]{2,1,0:T(8,128)S(1)} fusion(f32[2,2048,256]{2,1,0:T(8,128)} %bitcast.87, f32[2048,256]{1,0:T(8,128)S(1)} %shard_map.100, f32[2,256]{1,0:T(2,128)S(1)} %compare_convert_fusion), kind=kOutput, calls=%fused_computation.3 | convolution fusion | flops 3222274048 | bytes 6817792 | tf_op jit(solution)/shard_map/nk,tnl->tkl/dot_general | solution.py:135
  189.7 6.0 %shard_map.96 = f32[4096,256]{1,0:T(8,128)} custom-call(s32[8]{0:T(128)S(1)} %stack.96.refs_0_, s32[392,256]{1,0:T(8,128)S(1)} %shard_map.95.refs_1_, s32[392,256]{1,0:T(8,128)S(1)} %copy-done.5, s32[392,256]{1,0:T(8,128)S(1)} %copy-done.3, s32[392,256]{1,0:T(8,128)S(1)} %copy-done.1, s32[4,392,256]{2,1,0:T(8,128)} %collective-permute-done.6.refs_5_), custom_call_target="tpu_custom_call" | custom-call | bytes 7405600 | tf_op jit(solution)/shard_map/pallas_call | solution.py:145
  195.8 4.8 %collective-permute-done.17 = f32[512,256]{1,0:T(8,128)} collective-permute-done((f32[512,256]{1,0:T(8,128)}, f32[512,256]{1,0:T(8,128)}, u32[]{:S(2)}, u32[]{:S(2)}) %collective-permute-start.17) | collective-permute-done | bytes 524320 | tf_op jit(solution)/shard_map/ppermute | solution.py:127
  204.4 4.6 %subtract_multiply_fusion = f32[2,2048,256]{2,1,0:T(8,128)S(1)} fusion(f32[2,2048,256]{2,1,0:T(8,128)S(1)} %copy-done.20, f32[2,2048,256]{2,1,0:T(8,128)S(1)} %bitcast.82, f32[2,256,256]{2,1,0:T(8,128)S(1)} %fusion.28), kind=kOutput, calls=%fused_computation.2 | convolution fusion | flops 3223322624 | bytes 13107200 | tf_op jit(solution)/shard_map/tnk,tkl->tnl/dot_general | solution.py:135
  209.0 7.2 %convolution_add_fusion.gram_ref = f32[2,256,256]{2,1,0:T(8,128)S(1)} fusion(f32[2,2048,256]{2,1,0:T(8,128)S(1)} %subtract_multiply_fusion, f32[256,256]{1,0:T(8,128)S(1)} %copy-done.25, f32[2,256]{1,0:T(2,128)S(1)} %broadcast_subtract_fusion), kind=kOutput, calls=%fused_computation.24 | convolution fusion | flops 3221487616 | bytes 4982784 | tf_op jit(solution)/shard_map/tnk,tnl->tkl/dot_general | solution.py:135
  216.3 12.9 %shard_map.101 = f32[2,256,256]{2,1,0:T(8,128)S(1)} custom-call(f32[2,256,256]{2,1,0:T(8,128)S(1)} %convolution_add_fusion.gram_ref), custom_call_target="tpu_custom_call" | custom-call | tf_op jit(solution)/shard_map/pallas_call | solution.py:115
  229.1 4.4 %convolution_multiply_fusion = f32[2,2048,256]{2,1,0:T(8,128)S(1)} fusion(f32[2,2048,256]{2,1,0:T(8,128)S(1)} %subtract_multiply_fusion, f32[2,256,256]{2,1,0:T(8,128)S(1)} %shard_map.101), kind=kOutput, calls=%fused_computation.14 | convolution fusion | flops 3222274048 | bytes 8912896 | tf_op jit(solution)/shard_map/tnk,tlk->tnl/dot_general | solution.py:135
  233.6 7.0 %fusion.29 = f32[2,256,256]{2,1,0:T(8,128)S(1)} fusion(f32[2,2048,256]{2,1,0:T(8,128)S(1)} %bitcast.83, f32[2,2048,256]{2,1,0:T(8,128)S(1)} %convolution_multiply_fusion), kind=kOutput, calls=%fused_computation.49 | convolution fusion | flops 3221225472 | bytes 8912896 | tf_op jit(solution)/shard_map/tnk,tnl->tkl/dot_general | solution.py:135
  240.7 7.1 %fusion.8 = f32[2,256,256]{2,1,0:T(8,128)S(1)} fusion(f32[2,2048,256]{2,1,0:T(8,128)S(1)} %convolution_multiply_fusion, f32[2,2048,256]{2,1,0:T(8,128)S(1)} %bitcast.86, f32[2,256]{1,0:T(2,128)S(1)} %compare_convert_fusion), kind=kOutput, calls=%fused_computation.10 | convolution fusion | flops 3222274048 | bytes 8914944 | tf_op jit(solution)/shard_map/tnk,tnl->tkl/dot_general | solution.py:135
  248.9 4.3 %fusion.5 = f32[2,2048,256]{2,1,0:T(8,128)S(1)} fusion(f32[2,256,256]{2,1,0:T(8,128)S(1)} %fusion.8, f32[2,2048,256]{2,1,0:T(8,128)S(1)} %bitcast.90, f32[2,256]{1,0:T(2,128)S(1)} %compare_convert_fusion), kind=kOutput, calls=%fused_computation.7 | convolution fusion | flops 3222274048 | bytes 8914944 | tf_op jit(solution)/shard_map/tnk,tkl->tnl/dot_general | solution.py:135
  253.2 5.4 %fusion = f32[2,2048,256]{2,1,0:T(8,128)} fusion(f32[2,2048,256]{2,1,0:T(8,128)S(1)} %fusion.5, f32[2,256,256]{1,2,0:T(8,128)S(1)} %fusion.30, f32[2048,256]{1,0:T(8,128)S(1)} %shard_map.100), kind=kOutput, calls=%fused_computation.1 | convolution fusion | flops 3223322624 | bytes 11010048 | tf_op jit(solution)/shard_map/nk,tkl->tnl/dot_general | solution.py:135
  (104 shorter events, 34.0 us)
Async XLA Ops:
  0.6 52.4 %copy-start.7 = (f32[512,256]{1,0:T(8,128)S(1)}, f32[512,256]{1,0:T(8,128)}, u32[]{:S(2)}) copy-start(f32[512,256]{1,0:T(8,128)} %refs_6_.1) | copy-start | bytes 1572868
  0.6 30.3 %copy-start.14 = (bf16[64,2048]{1,0:T(8,128)(2,1)S(1)}, bf16[64,2048]{1,0:T(8,128)(2,1)}, u32[]{:S(2)}) copy-start(bf16[64,2048]{1,0:T(8,128)(2,1)} %refs_2_.1) | copy-start | bytes 786436
  0.7 52.4 %copy-start.15 = (s32[2]{0:T(128)S(1)}, s32[2]{0:T(128)}, u32[]{:S(2)}) copy-start(s32[2]{0:T(128)} %refs_1_.1) | copy-start | bytes 28
  0.7 17.0 %collective-permute-start.2 = (f32[512,256]{1,0:T(8,128)}, f32[512,256]{1,0:T(8,128)S(1)}, u32[]{:S(2)}, u32[]{:S(2)}) collective-permute-start(f32[512,256]{1,0:T(8,128)} %refs_6_.1), channel_id=1, source_target_pairs={{0,6},{1,7},{2,4},{3,5},{4,2},{5,3},{6,0},{7,1},{8,14},{9,15},{10,... | collective-permute-start | bytes 1572872 | tf_op jit(solution)/shard_map/ppermute | solution.py:127
  4.6 23.4 %collective-permute-start.1 = (f32[512,256]{1,0:T(8,128)}, f32[512,256]{1,0:T(8,128)S(1)}, u32[]{:S(2)}, u32[]{:S(2)}) collective-permute-start(f32[512,256]{1,0:T(8,128)} %refs_6_.1), channel_id=1, source_target_pairs={{0,4},{1,5},{2,6},{3,7},{4,0},{5,1},{6,2},{7,3},{8,12},{9,13},{10,... | collective-permute-start | bytes 1572872 | tf_op jit(solution)/shard_map/ppermute | solution.py:127
  5.1 23.2 %collective-permute-start = (f32[512,256]{1,0:T(8,128)}, f32[512,256]{1,0:T(8,128)S(1)}, u32[]{:S(2)}, u32[]{:S(2)}) collective-permute-start(f32[512,256]{1,0:T(8,128)} %refs_6_.1), channel_id=1, source_target_pairs={{0,2},{1,3},{2,0},{3,1},{4,6},{5,7},{6,4},{7,5},{8,10},{9,11},{10,... | collective-permute-start | bytes 1572872 | tf_op jit(solution)/shard_map/ppermute | solution.py:127
  28.3 37.7 %copy-start.6 = (f32[512,256]{1,0:T(8,128)S(1)}, f32[512,256]{1,0:T(8,128)}, u32[]{:S(2)}) copy-start(f32[512,256]{1,0:T(8,128)} %value_ref.1) | copy-start | bytes 1572868
  30.9 22.1 %collective-permute-start.10 = (f32[4,512,256]{2,1,0:T(8,128)}, f32[4,512,256]{2,1,0:T(8,128)}, u32[]{:S(2)}, u32[]{:S(2)}) collective-permute-start(f32[4,512,256]{2,1,0:T(8,128)} %pad_maximum_fusion), channel_id=1, source_target_pairs={{0,1},{1,0},{2,3},{3,2},{4,5},{5,4},{6,7},{7,6},{8,9},{9,8},{10,11... | collective-permute-start | bytes 6291464 | tf_op jit(solution)/shard_map/ppermute | solution.py:127
  30.9 15.7 %collective-permute-start.8 = (bf16[64,2048]{1,0:T(8,128)(2,1)S(1)}, bf16[64,2048]{1,0:T(8,128)(2,1)S(1)}, u32[]{:S(2)}, u32[]{:S(2)}) collective-permute-start(bf16[64,2048]{1,0:T(8,128)(2,1)S(1)} %copy-done.14), channel_id=1, source_target_pairs={{0,16},{8,24},{16,0},{24,8},{1,17},{9,25},{17,1},{25,9},{2,18},{10... | collective-permute-start | bytes 786440 | tf_op jit(solution)/shard_map/ppermute | solution.py:127
  33.5 13.1 %collective-permute-start.7 = (bf16[64,2048]{1,0:T(8,128)(2,1)S(1)}, bf16[64,2048]{1,0:T(8,128)(2,1)}, u32[]{:S(2)}, u32[]{:S(2)}) collective-permute-start(bf16[64,2048]{1,0:T(8,128)(2,1)S(1)} %copy-done.14), channel_id=1, source_target_pairs={{0,8},{8,0},{16,24},{24,16},{1,9},{9,1},{17,25},{25,17},{2,10},{10... | collective-permute-start | bytes 786440 | tf_op jit(solution)/shard_map/ppermute | solution.py:127
  35.1 18.0 %collective-permute-start.9 = (bf16[64,2048]{1,0:T(8,128)(2,1)S(1)}, bf16[64,2048]{1,0:T(8,128)(2,1)}, u32[]{:S(2)}, u32[]{:S(2)}) collective-permute-start(bf16[64,2048]{1,0:T(8,128)(2,1)S(1)} %copy-done.14), channel_id=1, source_target_pairs={{0,24},{8,16},{16,8},{24,0},{1,25},{9,17},{17,9},{25,1},{2,26},{10... | collective-permute-start | bytes 786440 | tf_op jit(solution)/shard_map/ppermute | solution.py:127
  58.3 67.0 %copy-start.26 = (s32[2,1]{0,1:T(1,128)S(1)}, s32[2,1]{0,1:T(1,128)}, u32[]{:S(2)}) copy-start(s32[2,1]{0,1:T(1,128)} %param.15) | copy-start | bytes 28
  58.3 14.6 %collective-permute-start.13 = (s32[200,512]{1,0:T(8,128)}, s32[200,512]{1,0:T(8,128)S(1)}, u32[]{:S(2)}, u32[]{:S(2)}) collective-permute-start(s32[200,512]{1,0:T(8,128)} %get-tuple-element.14), channel_id=1, source_target_pairs={{0,24},{8,16},{16,8},{24,0},{1,25},{9,17},{17,9},{25,1},{2,26},{10... | collective-permute-start | bytes 1228808 | tf_op jit(solution)/shard_map/ppermute | solution.py:127
  60.8 54.2 %collective-permute-start.12 = (s32[200,512]{1,0:T(8,128)}, s32[200,512]{1,0:T(8,128)S(1)}, u32[]{:S(2)}, u32[]{:S(2)}) collective-permute-start(s32[200,512]{1,0:T(8,128)} %get-tuple-element.14), channel_id=1, source_target_pairs={{0,16},{8,24},{16,0},{24,8},{1,17},{9,25},{17,1},{25,9},{2,18},{10... | collective-permute-start | bytes 1228808 | tf_op jit(solution)/shard_map/ppermute | solution.py:127
  65.5 50.3 %collective-permute-start.11 = (s32[200,512]{1,0:T(8,128)}, s32[200,512]{1,0:T(8,128)S(1)}, u32[]{:S(2)}, u32[]{:S(2)}) collective-permute-start(s32[200,512]{1,0:T(8,128)} %get-tuple-element.14), channel_id=1, source_target_pairs={{0,8},{8,0},{16,24},{24,16},{1,9},{9,1},{17,25},{25,17},{2,10},{10... | collective-permute-start | bytes 1228808 | tf_op jit(solution)/shard_map/ppermute | solution.py:127
  66.1 60.8 %collective-permute-start.20 = (s32[392,256]{1,0:T(8,128)S(1)}, s32[392,256]{1,0:T(8,128)S(1)}, u32[]{:S(2)}, u32[]{:S(2)}) collective-permute-start(s32[392,256]{1,0:T(8,128)S(1)} %shard_map.95.refs_1_), channel_id=1, source_target_pairs={{0,24},{8,16},{16,8},{24,0},{1,25},{9,17},{17,9},{25,1},{2,26},{10... | collective-permute-start | bytes 1204232 | tf_op jit(solution)/shard_map/ppermute | solution.py:127
  68.6 63.6 %collective-permute-start.19 = (s32[392,256]{1,0:T(8,128)S(1)}, s32[392,256]{1,0:T(8,128)S(1)}, u32[]{:S(2)}, u32[]{:S(2)}) collective-permute-start(s32[392,256]{1,0:T(8,128)S(1)} %shard_map.95.refs_1_), channel_id=1, source_target_pairs={{0,16},{8,24},{16,0},{24,8},{1,17},{9,25},{17,1},{25,9},{2,18},{10... | collective-permute-start | bytes 1204232 | tf_op jit(solution)/shard_map/ppermute | solution.py:127
  73.7 60.0 %collective-permute-start.18 = (s32[392,256]{1,0:T(8,128)S(1)}, s32[392,256]{1,0:T(8,128)}, u32[]{:S(2)}, u32[]{:S(2)}) collective-permute-start(s32[392,256]{1,0:T(8,128)S(1)} %shard_map.95.refs_1_), channel_id=1, source_target_pairs={{0,8},{8,0},{16,24},{24,16},{1,9},{9,1},{17,25},{25,17},{2,10},{10... | collective-permute-start | bytes 1204232 | tf_op jit(solution)/shard_map/ppermute | solution.py:127
  125.1 46.2 %collective-permute-start.14 = (f32[4,512,256]{2,1,0:T(8,128)}, f32[4,512,256]{2,1,0:T(8,128)}, u32[]{:S(2)}, u32[]{:S(2)}) collective-permute-start(f32[4,512,256]{2,1,0:T(8,128)} %get-tuple-element.16), channel_id=1, source_target_pairs={{0,1},{1,0},{2,3},{3,2},{4,5},{5,4},{6,7},{7,6},{8,9},{9,8},{10,11... | collective-permute-start | bytes 6291464 | tf_op jit(solution)/shard_map/ppermute | solution.py:127
  125.3 20.2 %collective-permute-start.5 = (s32[392,256]{1,0:T(8,128)S(1)}, s32[392,256]{1,0:T(8,128)S(1)}, u32[]{:S(2)}, u32[]{:S(2)}) collective-permute-start(s32[392,256]{1,0:T(8,128)S(1)} %shard_map.95.refs_1_), channel_id=1, source_target_pairs={{0,6},{1,7},{2,4},{3,5},{4,2},{5,3},{6,0},{7,1},{8,14},{9,15},{10,... | collective-permute-start | bytes 1204232 | tf_op jit(solution)/shard_map/ppermute | solution.py:127
  127.0 19.6 %collective-permute-start.4 = (s32[392,256]{1,0:T(8,128)S(1)}, s32[392,256]{1,0:T(8,128)S(1)}, u32[]{:S(2)}, u32[]{:S(2)}) collective-permute-start(s32[392,256]{1,0:T(8,128)S(1)} %shard_map.95.refs_1_), channel_id=1, source_target_pairs={{0,4},{1,5},{2,6},{3,7},{4,0},{5,1},{6,2},{7,3},{8,12},{9,13},{10,... | collective-permute-start | bytes 1204232 | tf_op jit(solution)/shard_map/ppermute | solution.py:127
  132.2 15.9 %collective-permute-start.3 = (s32[392,256]{1,0:T(8,128)S(1)}, s32[392,256]{1,0:T(8,128)S(1)}, u32[]{:S(2)}, u32[]{:S(2)}) collective-permute-start(s32[392,256]{1,0:T(8,128)S(1)} %shard_map.95.refs_1_), channel_id=1, source_target_pairs={{0,2},{1,3},{2,0},{3,1},{4,6},{5,7},{6,4},{7,5},{8,10},{9,11},{10,... | collective-permute-start | bytes 1204232 | tf_op jit(solution)/shard_map/ppermute | solution.py:127
  135.7 28.0 %collective-permute-start.21 = (s32[392,256]{1,0:T(8,128)S(1)}, s32[392,256]{1,0:T(8,128)S(1)}, u32[]{:S(2)}, u32[]{:S(2)}) collective-permute-start(s32[392,256]{1,0:T(8,128)S(1)} %get-tuple-element.18), channel_id=1, source_target_pairs={{0,4},{1,5},{2,6},{3,7},{4,0},{5,1},{6,2},{7,3},{8,12},{9,13},{10,... | collective-permute-start | bytes 1204232 | tf_op jit(solution)/shard_map/ppermute | solution.py:127
  145.5 20.8 %copy-start.21 = (f32[4096,256]{1,0:T(8,128)S(1)}, f32[4096,256]{1,0:T(8,128)}, u32[]{:S(2)}) copy-start(f32[4096,256]{1,0:T(8,128)} %param.12) | copy-start | bytes 12582916
  145.5 18.2 %collective-permute-start.22 = (s32[392,256]{1,0:T(8,128)S(1)}, s32[392,256]{1,0:T(8,128)S(1)}, u32[]{:S(2)}, u32[]{:S(2)}) collective-permute-start(s32[392,256]{1,0:T(8,128)S(1)} %get-tuple-element.20), channel_id=1, source_target_pairs={{0,6},{1,7},{2,4},{3,5},{4,2},{5,3},{6,0},{7,1},{8,14},{9,15},{10,... | collective-permute-start | bytes 1204232 | tf_op jit(solution)/shard_map/ppermute | solution.py:127
  146.6 18.7 %copy-start.2 = (s32[392,256]{1,0:T(8,128)}, s32[392,256]{1,0:T(8,128)S(1)}, u32[]{:S(2)}) copy-start(s32[392,256]{1,0:T(8,128)S(1)} %collective-permute-done.4.refs_3_) | copy-start | bytes 1204228
  146.6 18.7 %collective-permute-start.23 = (s32[392,256]{1,0:T(8,128)S(1)}, s32[392,256]{1,0:T(8,128)S(1)}, u32[]{:S(2)}, u32[]{:S(2)}) collective-permute-start(s32[392,256]{1,0:T(8,128)S(1)} %get-tuple-element.21), channel_id=1, source_target_pairs={{0,2},{1,3},{2,0},{3,1},{4,6},{5,7},{6,4},{7,5},{8,10},{9,11},{10,... | collective-permute-start | bytes 1204232 | tf_op jit(solution)/shard_map/ppermute | solution.py:127
  149.4 40.3 %collective-permute-start.6 = (s32[4,392,256]{2,1,0:T(8,128)}, s32[4,392,256]{2,1,0:T(8,128)}, u32[]{:S(2)}, u32[]{:S(2)}) collective-permute-start(s32[4,392,256]{2,1,0:T(8,128)} %pad_add_fusion), channel_id=1, source_target_pairs={{0,1},{1,0},{2,3},{3,2},{4,5},{5,4},{6,7},{7,6},{8,9},{9,8},{10,11... | collective-permute-start | bytes 4816904 | tf_op jit(solution)/shard_map/ppermute | solution.py:127
  166.3 12.1 %collective-permute-start.24 = (s32[2,392,256]{2,1,0:T(8,128)}, s32[2,392,256]{2,1,0:T(8,128)}, u32[]{:S(2)}, u32[]{:S(2)}) collective-permute-start(s32[2,392,256]{2,1,0:T(8,128)} %pad_add_fusion.1), channel_id=1, source_target_pairs={{0,1},{1,0},{2,3},{3,2},{4,5},{5,4},{6,7},{7,6},{8,9},{9,8},{10,11... | collective-permute-start | bytes 2408456 | tf_op jit(solution)/shard_map/ppermute | solution.py:127
  174.0 21.8 %collective-permute-start.15 = (f32[512,256]{1,0:T(8,128)}, f32[512,256]{1,0:T(8,128)}, u32[]{:S(2)}, u32[]{:S(2)}) collective-permute-start(f32[512,256]{1,0:T(8,128)} %get-tuple-element.22), channel_id=1, source_target_pairs={{0,2},{1,3},{2,0},{3,1},{4,6},{5,7},{6,4},{7,5},{8,10},{9,11},{10,... | collective-permute-start | bytes 1572872 | tf_op jit(solution)/shard_map/ppermute | solution.py:127
  174.4 26.1 %collective-permute-start.17 = (f32[512,256]{1,0:T(8,128)}, f32[512,256]{1,0:T(8,128)}, u32[]{:S(2)}, u32[]{:S(2)}) collective-permute-start(f32[512,256]{1,0:T(8,128)} %get-tuple-element.23), channel_id=1, source_target_pairs={{0,6},{1,7},{2,4},{3,5},{4,2},{5,3},{6,0},{7,1},{8,14},{9,15},{10,... | collective-permute-start | bytes 1572872 | tf_op jit(solution)/shard_map/ppermute | solution.py:127
  176.6 25.3 %collective-permute-start.16 = (f32[512,256]{1,0:T(8,128)}, f32[512,256]{1,0:T(8,128)}, u32[]{:S(2)}, u32[]{:S(2)}) collective-permute-start(f32[512,256]{1,0:T(8,128)} %get-tuple-element.24), channel_id=1, source_target_pairs={{0,4},{1,5},{2,6},{3,7},{4,0},{5,1},{6,2},{7,3},{8,12},{9,13},{10,... | collective-permute-start | bytes 1572872 | tf_op jit(solution)/shard_map/ppermute | solution.py:127
  (20 other events, 149.2 us)

commit v2 on v1

--- a/solution.py
+++ b/solution.py
@@ -139,7 +139,7 @@
     return jax.ShapeDtypeStruct(shape, dtype)
 
 
-def call(kernel, out, args, kinds, scratch=(), limit=48, flops=0):
+def call(kernel, out, args, kinds, scratch=(), limit=60, flops=0):
     spaces = {"v": pltpu.VMEM, "s": pltpu.SMEM, "a": pl.ANY}
     moved = sum(a.size * a.dtype.itemsize for a in [*out, *args])
     return pl.pallas_call(
@@ -205,8 +205,8 @@
 
 
 def solve_kernel(rows, pairs, where_ref, rank_ref, *refs):
-    inverse, held, other = refs[:rows], refs[rows : rows + pairs], refs[rows + pairs]
-    out_ref, packed_ref, whole, right, sem = refs[rows + pairs + 1 :]
+    inverse, held, other = refs[:rows], refs[rows : rows + pairs], refs[rows + pairs : rows + 2 * pairs]
+    out_ref, packed_ref, whole, right, sem = refs[rows + 2 * pairs :]
     floor, me = where_ref[0], where_ref[1]
     part = inverse[0].shape[0]
     chunk, cap = held[0].shape
@@ -216,7 +216,7 @@
         (inverse[d], whole.at[pl.ds(pl.multiple_of((floor ^ d) * part, part), part), :]) for d in range(rows)
     ]
     for at in range(2 * pairs):
-        moves.append((held[at // 2] if at % 2 == 0 else other.at[at // 2], right.at[at]))
+        moves.append((held[at // 2] if at % 2 == 0 else other[at // 2], right.at[at]))
     load_all(moves, sem)
     column = lax.broadcasted_iota(jnp.int32, (1, cap), 1)
     for h in range(2):
@@ -246,8 +246,10 @@
 
     own_high, own_low = halves(own)
 
+    own_high, own_low = own_high.T, own_low.T
+
     def across(x, y):
-        return lax.dot_general(x, y, (((0,), (0,)), ((), ())), preferred_element_type=jnp.float32)
+        return jnp.dot(x, y, preferred_element_type=jnp.float32)
 
     for e in range(pairs):
         wanted = floor ^ pair ^ e
@@ -260,39 +262,36 @@
 
 
 def choose_kernel(rows, pairs, where_ref, *refs):
-    ins, outs, sem = refs[:rows], refs[rows : rows + pairs], refs[rows + pairs]
+    ins, outs = refs[:rows], refs[rows:]
     mark = where_ref[0] ^ (where_ref[1] // 2)
-    for g in range(rows):
-
-        @pl.when(mark == g)
-        def _(g=g):
-            load_all([(ins[g ^ e], outs[e]) for e in range(pairs)], sem)
-
-
-def spread_kernel(count, slot_ref, *refs):
-    blocks, (out_ref, words, sem) = refs[:-3], refs[-3:]
-    flat = []
-    for b in blocks:
-        flat += [b] if len(b.shape) == 2 else [b.at[i] for i in range(b.shape[0])]
-    load_all([(flat[n], words.at[n]) for n in range(count)], sem)
-    for n in range(count):
-        values = unpack(words[n])
+    for e in range(pairs):
+        outs[e][0] = ins[0][...]
+        for d in range(rows):
+
+            @pl.when(mark == d ^ e)
+            def _(d=d, e=e):
+                outs[e][1] = ins[d][...]
+
+
+def spread_kernel(pairs, where_ref, *refs):
+    held, other, (row_ref, col_ref, words, sem) = refs[:pairs], refs[pairs : 2 * pairs], refs[2 * pairs :]
+    me = where_ref[1]
+    pair, side = me // 2, me % 2
+    half = pairs // 2
+    load_all([(ref, words.at[n]) for n, ref in enumerate([*held, *other])], sem)
+
+    def put(ref, values, slot):
         piece = values[0].shape[0]
         for i in range(4):
-            at = pl.multiple_of(slot_ref[n] * (4 * piece) + piece * i, piece)
-            out_ref[pl.ds(at, piece), :] = values[i]
-
-
-def spread(slots, blocks, count):
-    words, width = blocks[0].shape[-2:]
-    chunk = (words - 8) // 3 * 4
-    return call(
-        lambda *refs: spread_kernel(count, *refs),
-        [shaped((count * chunk, width))],
-        [jnp.stack(slots), *blocks],
-        "s" + "a" * len(blocks) + "v",
-        [pltpu.VMEM((count, words, width), jnp.int32), pltpu.SemaphoreType.DMA((count,))],
-    )[0]
+            ref[pl.ds(pl.multiple_of(slot * (4 * piece) + piece * i, piece), piece), :] = values[i]
+
+    for n in range(2 * pairs):
+        put(row_ref, unpack(words[n, 0]), me ^ (2 * (n % pairs) + n // pairs))
+    upper = (pair // half) ^ side
+    for n in range(pairs):
+        e = n % half + half * upper
+        from_other = n // half
+        put(col_ref, unpack(words[from_other * pairs + e, 1]), 2 * ((pair ^ e) % half) + (side ^ from_other))
 
 
 def make_shards(rows, cols):
@@ -312,21 +311,18 @@
         my_pair, my_side = me // 2, me % 2
         wide = tile_rows * rank_cap
 
+        words = call(pack_kernel, [shaped((packed_rows(chunk), rank_cap), jnp.int32)], [panel_left], "vv")[0]
         inverse = [factor_inverse] + [flip(factor_inverse, "row", rows, d) for d in range(1, rows)]
-        held = [panel_right] + [flip(panel_right, "col", cols, 2 * d) for d in range(1, pairs)]
-        other = flip(jnp.stack(held), "col", cols, 1)
-
-        words = call(pack_kernel, [shaped((packed_rows(chunk), rank_cap), jnp.int32)], [panel_left], "vv")[0]
-        words_z = after(words, *inverse[1:])
-        from_floors = [words_z] + [flip(words_z, "row", rows, d) for d in range(1, rows)]
-        words_p = after(words, *held[1:])
-        row_held = [words_p] + [flip(words_p, "col", cols, 2 * d) for d in range(1, pairs)]
+        held = [panel_right] + [flip(panel_right, "col", cols, 2 * e) for e in range(1, pairs)]
+        held, inverse, words = lax.optimization_barrier((held, inverse, words))
+        other = [flip(h, "col", cols, 1) for h in held]
+        from_floors = [words] + [flip(words, "row", rows, d) for d in range(1, rows)]
 
         solved, solved_words = call(
             lambda *refs: solve_kernel(rows, pairs, *refs),
             [shaped((rows * part, wide)), shaped((packed_rows(rows * part), wide), jnp.int32)],
-            [spot, panel_rank, *inverse, *held, other],
-            "ss" + "a" * (rows + pairs + 1) + "vv",
+            [spot, panel_rank, *inverse, *held, *other],
+            "ss" + "a" * (rows + 2 * pairs) + "vv",
             [
                 pltpu.VMEM((rows * part, tile_order), jnp.bfloat16),
                 pltpu.VMEM((cols, chunk, rank_cap), jnp.float32),
@@ -336,33 +332,27 @@
         )
         arrived = [flip(solved_words, "row", rows, d) for d in range(1, rows)]
 
-        row_other = flip(jnp.stack(row_held), "col", cols, 1)
-        row_left = spread(
-            [me ^ (2 * d) for d in range(pairs)] + [me ^ (2 * d + 1) for d in range(pairs)],
-            [*row_held, row_other],
-            cols,
-        ).reshape(tile_rows, tile_order, rank_cap)
-
-        got = call(
+        *from_floors, _ = lax.optimization_barrier((*from_floors, solved_words))
+        mixed = call(
             lambda *refs: choose_kernel(rows, pairs, *refs),
-            [shaped(words.shape, jnp.int32)] * pairs,
+            [shaped((2, *words.shape), jnp.int32)] * pairs,
             [spot, *from_floors],
-            "s" + "a" * (rows + pairs),
-            [pltpu.SemaphoreType.DMA((pairs,))],
+            "s" + "v" * (rows + pairs),
         )
-        got = [flip(got[d], "col", cols, 2 * d) if d else got[d] for d in range(pairs)]
-        half = pairs // 2
-        top = my_pair // half
-        upper = (top ^ my_side) == 1
-        keep = [jnp.where(upper, got[half + d], got[d]) for d in range(half)]
-        give = [jnp.where(upper, got[d], got[half + d]) for d in range(half)]
-        take = flip(jnp.stack(give), "col", cols, 1)
-        low = my_pair % half
-        col_left = spread(
-            [2 * (low ^ d) + my_side for d in range(half)] + [2 * (low ^ d) + 1 - my_side for d in range(half)],
-            [*keep, take],
-            pairs,
-        )
+        mixed = [flip(mixed[e], "col", cols, 2 * e) if e else mixed[e] for e in range(pairs)]
+
+        kept_cols = (columns[None, :] < trail_rank).astype(jnp.float32)[:, None, :]
+
+        def to_tiles(block):
+            return block.reshape(tile_rows, tile_order, rank_cap) * kept_cols
+
+        tile_left = to_tiles(left)
+        tile_right = to_tiles(right)
+        tile_probe = to_tiles(probes)
+        right_probe = dot("tnk,tnl->tkl", tile_right, tile_probe)
+        tile_part = dot("tnk,tkl->tnl", tile_left, right_probe)
+        mixed, arrived, tile_part = lax.optimization_barrier((mixed, arrived, tile_part))
+        swapped = [flip(m, "col", cols, 1) for m in mixed]
 
         mine, theirs = call(
             lambda *refs: core_kernel(rows, pairs, *refs),
@@ -377,20 +367,20 @@
         )
         theirs = flip(theirs, "col", cols, 1)
         parts = [mine[e] + theirs[e] for e in range(pairs)]
-        panel_core = sum(flip(parts[e], "col", cols, 2 * e) if e else parts[e] for e in range(pairs))
-        panel_core = panel_core.reshape(tile_rows, rank_cap, rank_cap) / tile_order
-
-        kept_cols = (columns[None, :] < trail_rank).astype(jnp.float32)[:, None, :]
-
-        def to_tiles(block):
-            return block.reshape(tile_rows, tile_order, rank_cap) * kept_cols
-
-        tile_left = to_tiles(left)
-        tile_right = to_tiles(right)
-        tile_probe = to_tiles(probes)
-        right_probe = dot("tnk,tnl->tkl", tile_right, tile_probe)
-        tile_part = dot("tnk,tkl->tnl", tile_left, right_probe)
+        swapped = lax.optimization_barrier((swapped, parts))[0]
+        parts = [flip(parts[e], "col", cols, 2 * e) if e else parts[e] for e in range(pairs)]
+        row_left, col_left = call(
+            lambda *refs: spread_kernel(pairs, *refs),
+            [shaped((cols * chunk, rank_cap)), shaped((pairs * chunk, rank_cap))],
+            [spot, *mixed, *swapped],
+            "s" + "a" * (2 * pairs) + "vv",
+            [pltpu.VMEM((2 * pairs, 2, *words.shape), jnp.int32), pltpu.SemaphoreType.DMA((2 * pairs,))],
+        )
+        row_left = row_left.reshape(tile_rows, tile_order, rank_cap)
+
         panel_probe = dot("nk,tnl->tkl", col_left, tile_probe)
+        parts, panel_probe, row_left = lax.optimization_barrier((parts, panel_probe, row_left))
+        panel_core = sum(parts).reshape(tile_rows, rank_cap, rank_cap) / tile_order
         core_probe = dot("tkl,tlm->tkm", panel_core, panel_probe)
         sampled = (tile_part - dot("tnk,tkl->tnl", row_left, core_probe)) / tile_order
         identity = (columns[:, None] == columns[None, :]).astype(jnp.float32)

time: 264 us -> 224 us (0.85)
  starting transfers between devices: 49.2 us -> 29.2 us
  waiting for transfers between devices: 93.9 us -> 75.2 us
  Pallas kernels: 33.3 us -> 38.9 us
  other arithmetic: 10.4 us -> 5.31 us
  local copies, waits for them, and re-layouts: 6.52 us -> 3.5 us
    ppermute x25 -> x27, starting transfers between devices: 49.2 us -> 29.2 us  [flip(): return lax.ppermute(value, axis, [(i, i ^ mask) for i in range(size)])]
    ppermute x25 -> x27, waiting for transfers between devices: 93.9 us -> 75.2 us  [flip(): return lax.ppermute(value, axis, [(i, i ^ mask) for i in range(size)])]
    pallas_call x6 -> x5, Pallas kernels: 20.4 us -> 25.8 us  [call(): pl.pallas_call(kernel, out_shape=out, in_specs=[pl.BlockSpec(memory_space...]
    another operation x6 -> x0, other arithmetic: 5.08 us -> none  [the longest x1 2.62 us: shards(): other = flip(jnp.stack(held), 'col', cols, 1)]
    unnamed x54 -> x60, local copies, waits for them, and re-layouts: 6.44 us -> 3.5 us
  transfers between devices with their start and end apart: 25 -> 27, of which waited for: 13 -> 12; matrix products, arithmetic and copies ran while one was open for 11% -> 13% of each run, Pallas kernels for 6% -> 9%
where the time goes in v2:
time: 224 us; the launch traced here: 220 us
  waiting for transfers between devices  75.2 us (34%)
  matrix products  66.4 us (30%)
  Pallas kernels  38.9 us (17%)
  starting transfers between devices  29.2 us (13%)
  other arithmetic  5.31 us (2%)
  local copies, waits for them, and re-layouts  3.5 us (2%)
    ppermute x27, waiting for transfers between devices, flip(): return lax.ppermute(value, axis, [(i, i ^ mask) for i in range(size)])  75.2 us
    dot_general x12, matrix products, dot(): jnp.einsum(spec, a, b, precision=highest, preferred_element_type=jnp.floa...  66.4 us
    ppermute x27, starting transfers between devices, flip(): return lax.ppermute(value, axis, [(i, i ^ mask) for i in range(size)])  29.2 us
    pallas_call x5, Pallas kernels, call(): pl.pallas_call(kernel, out_shape=out, in_specs=[pl.BlockSpec(memory_space...  25.8 us
    pallas_call x1, Pallas kernels, factor(): pl.pallas_call(factor_kernel, out_shape=jax.ShapeDtypeStruct(gram.shape,...  13.1 us
  transfers between devices with their start and end apart: 27, of which 12 were waited for; matrix products, arithmetic and copies ran while one was open for 13% of the time, Pallas kernels for 9%

profile of v2, /device:TPU:0, one launch (start us, length us, event | category | flops | bytes accessed | tf_op | source)
XLA Modules:
  0.0 220.0 jit_solution(16385785339593340689)
XLA Ops:
  0.6 4.1 %collective-permute-start.4 = (bf16[64,2048]{1,0:T(8,128)(2,1)}, bf16[64,2048]{1,0:T(8,128)(2,1)}, u32[]{:S(2)}, u32[]{:S(2)}) collective-permute-start(bf16[64,2048]{1,0:T(8,128)(2,1)} %refs_2_), channel_id=1, source_target_pairs={{0,16},{8,24},{16,0},{24,8},{1,17},{9,25},{17,1},{25,9},{2,18},{10... | collective-permute-start | bytes 786440 | tf_op jit(solution)/shard_map/ppermute | solution.py:127
  4.7 1.5 collective-permute-start.1
  8.2 1.6 collective-permute-start.3
  9.8 7.3 %collective-permute-done.4.refs_4_ = bf16[64,2048]{1,0:T(8,128)(2,1)} collective-permute-done((bf16[64,2048]{1,0:T(8,128)(2,1)}, bf16[64,2048]{1,0:T(8,128)(2,1)}, u32[]{:S(2)}, u32[]{:S(2)}) %collective-permute-start.4) | collective-permute-done | bytes 262176 | tf_op jit(solution)/shard_map/ppermute | solution.py:127
  17.1 3.5 %collective-permute-start.5 = (bf16[64,2048]{1,0:T(8,128)(2,1)}, bf16[64,2048]{1,0:T(8,128)(2,1)S(1)}, u32[]{:S(2)}, u32[]{:S(2)}) collective-permute-start(bf16[64,2048]{1,0:T(8,128)(2,1)} %refs_2_), channel_id=1, source_target_pairs={{0,24},{8,16},{16,8},{24,0},{1,25},{9,17},{17,9},{25,1},{2,26},{10... | collective-permute-start | bytes 786440 | tf_op jit(solution)/shard_map/ppermute | solution.py:127
  20.6 2.0 shard_map.95.refs_1_
  22.6 4.8 %collective-permute-done.5.refs_5_ = bf16[64,2048]{1,0:T(8,128)(2,1)S(1)} collective-permute-done((bf16[64,2048]{1,0:T(8,128)(2,1)}, bf16[64,2048]{1,0:T(8,128)(2,1)S(1)}, u32[]{:S(2)}, u32[]{:S(2)}) %collective-permute-start.5) | collective-permute-done | bytes 262176 | tf_op jit(solution)/shard_map/ppermute | solution.py:127
  27.4 3.4 %collective-permute-done.2.refs_9_ = f32[512,256]{1,0:T(8,128)S(1)} collective-permute-done((f32[512,256]{1,0:T(8,128)}, f32[512,256]{1,0:T(8,128)S(1)}, u32[]{:S(2)}, u32[]{:S(2)}) %collective-permute-start.2) | collective-permute-done | bytes 524320 | tf_op jit(solution)/shard_map/ppermute | solution.py:127
  37.5 6.1 %shard_map.96 = (f32[256,512]{1,0:T(8,128)}, s32[200,512]{1,0:T(8,128)}) custom-call(s32[2]{0:T(128)} %pad_add_fusion.refs_0_, s32[2]{0:T(128)} %refs_1_.1, bf16[64,2048]{1,0:T(8,128)(2,1)} %refs_2_, bf16[64,2048]{1,0:T(8,128)(2,1)} %copy-done.28, bf16[64,2048]{1,0:T(8,128)(2,1)} %collective-permute-done.4.refs_4_, bf16[64,2048]{1,0:T(8,128)(2,1)} %copy-done.29, ...), custom_call_target="tpu_custom_call" | custom-call | flops 1610612736 | bytes 6176784 | tf_op jit(solution)/shard_map/pallas_call | solution.py:145
  43.6 1.9 collective-permute-start.18
  46.1 33.6 %collective-permute-done.7.refs_3_ = s32[392,256]{1,0:T(8,128)S(1)} collective-permute-done((s32[392,256]{1,0:T(8,128)}, s32[392,256]{1,0:T(8,128)S(1)}, u32[]{:S(2)}, u32[]{:S(2)}) %collective-permute-start.7) | collective-permute-done | bytes 401440 | tf_op jit(solution)/shard_map/ppermute | solution.py:127
  81.2 3.6 %shard_map.97 = (s32[2,392,256]{2,1,0:T(8,128)}, s32[2,392,256]{2,1,0:T(8,128)}, s32[2,392,256]{2,1,0:T(8,128)}, s32[2,392,256]{2,1,0:T(8,128)}) custom-call(s32[2]{0:T(128)} %pad_add_fusion.refs_0_, s32[392,256]{1,0:T(8,128)} %shard_map.95.refs_1_, s32[392,256]{1,0:T(8,128)} %copy-done.17, s32[392,256]{1,0:T(8,128)} %copy-done.16, s32[392,256]{1,0:T(8,128)} %copy-done.15), custom_call_target="tpu_custom_call" | custom-call | bytes 4816904 | tf_op jit(solution)/shard_map/pallas_call | solution.py:145
  86.3 1.5 collective-permute-start.14
  88.3 10.6 %fusion.3 = f32[2,256,256]{2,1,0:T(8,128)S(1)} fusion(f32[2,2048,256]{2,1,0:T(8,128)} %bitcast.47, f32[2,2048,256]{2,1,0:T(8,128)} %bitcast.49, f32[2,256]{1,0:T(2,128)S(1)} %compare_convert_fusion), kind=kOutput, calls=%fused_computation.5 | convolution fusion | flops 3223322624 | bytes 8914944 | tf_op jit(solution)/shard_map/tnk,tnl->tkl/dot_general | solution.py:135
  100.4 5.0 %fusion.10 = f32[2,2048,256]{2,1,0:T(8,128)} fusion(f32[2,256,256]{2,1,0:T(8,128)S(1)} %fusion.3, f32[2,2048,256]{2,1,0:T(8,128)S(1)} %bitcast.45, f32[2,256]{1,0:T(2,128)S(1)} %compare_convert_fusion), kind=kOutput, calls=%fused_computation.12 | convolution fusion | flops 3222274048 | bytes 8914944 | tf_op jit(solution)/shard_map/tnk,tkl->tnl/dot_general | solution.py:135
  105.4 11.1 %collective-permute-done.17.refs_3_ = s32[200,512]{1,0:T(8,128)S(1)} collective-permute-done((s32[200,512]{1,0:T(8,128)S(1)}, s32[200,512]{1,0:T(8,128)S(1)}, u32[]{:S(2)}, u32[]{:S(2)}) %collective-permute-start.17) | collective-permute-done | bytes 409632 | tf_op jit(solution)/shard_map/ppermute | solution.py:127
  116.7 4.8 %collective-permute-done.14.refs_3_ = s32[2,392,256]{2,1,0:T(8,128)S(1)} collective-permute-done((s32[2,392,256]{2,1,0:T(8,128)}, s32[2,392,256]{2,1,0:T(8,128)S(1)}, u32[]{:S(2)}, u32[]{:S(2)}) %collective-permute-start.14) | collective-permute-done | bytes 802848 | tf_op jit(solution)/shard_map/ppermute | solution.py:127
  121.6 6.7 %shard_map.98 = (f32[4,512,256]{2,1,0:T(8,128)}, f32[4,512,256]{2,1,0:T(8,128)}) custom-call(s32[2]{0:T(128)} %pad_add_fusion.refs_0_, f32[256,512]{1,0:T(8,128)} %get-tuple-element.62.refs_1_, s32[200,512]{1,0:T(8,128)} %copy-done.27, s32[200,512]{1,0:T(8,128)} %copy-done.26, s32[200,512]{1,0:T(8,128)} %copy-done.24), custom_call_target="tpu_custom_call" | custom-call | flops 1610612736 | bytes 5947400 | tf_op jit(solution)/shard_map/pallas_call | solution.py:145
  129.5 5.4 %collective-permute-done.19 = f32[4,512,256]{2,1,0:T(8,128)S(1)} collective-permute-done((f32[4,512,256]{2,1,0:T(8,128)}, f32[4,512,256]{2,1,0:T(8,128)S(1)}, u32[]{:S(2)}, u32[]{:S(2)}) %collective-permute-start.19) | collective-permute-done | bytes 2097184 | tf_op jit(solution)/shard_map/ppermute | solution.py:127
  134.9 2.8 %fusion.29 = (f32[512,256]{1,0:T(8,128)}, f32[512,256]{1,0:T(8,128)}, f32[512,256]{1,0:T(8,128)}, f32[512,256]{1,0:T(8,128)S(1)}) fusion(f32[4,512,256]{2,1,0:T(8,128)S(1)} %collective-permute-done.19, f32[4,512,256]{2,1,0:T(8,128)} %get-tuple-element.66), kind=kLoop, calls=%fused_computation.27 | loop fusion | flops 524288 | bytes 6291456 | tf_op jit(solution)/shard_map/add | solution.py:369
  137.7 1.6 collective-permute-start.22
  143.3 7.5 %shard_map.99 = (f32[4096,256]{1,0:T(8,128)}, f32[2048,256]{1,0:T(8,128)}) custom-call(s32[2]{0:T(128)} %pad_add_fusion.refs_0_, s32[2,392,256]{2,1,0:T(8,128)} %get-tuple-element.68.refs_1_, s32[2,392,256]{2,1,0:T(8,128)} %copy-done.8, s32[2,392,256]{2,1,0:T(8,128)} %copy-done.9, s32[2,392,256]{2,1,0:T(8,128)} %copy-done.10, s32[2,392,256]{2,1,0:T(8,128)} %copy-done.11, ...), custom_call_target="tpu_custom_call" | custom-call | bytes 12713992 | tf_op jit(solution)/shard_map/pallas_call | solution.py:145
  150.8 9.9 %fusion.23 = f32[2,256,256]{1,2,0:T(8,128)S(1)} fusion(f32[2048,256]{1,0:T(8,128)} %get-tuple-element.76, f32[2,2048,256]{2,1,0:T(8,128)} %bitcast.48, f32[2,256]{1,0:T(2,128)S(1)} %compare_convert_fusion), kind=kOutput, calls=%fused_computation.24 | convolution fusion | flops 3222274048 | bytes 6817792 | tf_op jit(solution)/shard_map/nk,tnl->tkl/dot_general | solution.py:135
  160.7 3.3 %collective-permute-done.21 = f32[512,256]{1,0:T(8,128)S(1)} collective-permute-done((f32[512,256]{1,0:T(8,128)}, f32[512,256]{1,0:T(8,128)S(1)}, u32[]{:S(2)}, u32[]{:S(2)}) %collective-permute-start.21) | collective-permute-done | bytes 524320 | tf_op jit(solution)/shard_map/ppermute | solution.py:127
  166.0 4.2 %fusion.37 = f32[2,2048,256]{2,1,0:T(8,128)S(1)} fusion(f32[2,2048,256]{2,1,0:T(8,128)S(1)} %bitcast.51, f32[2,256,256]{2,1,0:T(8,128)S(1)} %fusion.36), kind=kOutput, calls=%fused_computation.43 | convolution fusion | flops 3221225472 | bytes 8912896 | tf_op jit(solution)/shard_map/tnk,tkl->tnl/dot_general | solution.py:135
  170.3 7.2 %fusion.28.gram_ref = f32[2,256,256]{2,1,0:T(8,128)S(1)} fusion(f32[2,2048,256]{2,1,0:T(8,128)S(1)} %copy-done, f32[2,2048,256]{2,1,0:T(8,128)S(1)} %fusion.37, f32[256,256]{1,0:T(8,128)S(1)} %fusion.33, f32[2,256]{1,0:T(2,128)S(1)} %broadcast_subtract_fusion), kind=kOutput, calls=%fused_computation.25 | convolution fusion | flops 3223584768 | bytes 9177088 | tf_op jit(solution)/shard_map/tnk,tnl->tkl/dot_general | solution.py:135
  177.4 13.1 %shard_map.100 = f32[2,256,256]{2,1,0:T(8,128)S(1)} custom-call(f32[2,256,256]{2,1,0:T(8,128)S(1)} %fusion.28.gram_ref), custom_call_target="tpu_custom_call" | custom-call | tf_op jit(solution)/shard_map/pallas_call | solution.py:115
  190.5 4.8 %convolution_multiply_fusion = f32[2,2048,256]{2,1,0:T(8,128)S(1)} fusion(f32[2,256,256]{2,1,0:T(8,128)S(1)} %shard_map.100, f32[2,2048,256]{2,1,0:T(8,128)S(1)} %copy-done, f32[2,2048,256]{2,1,0:T(8,128)S(1)} %fusion.37), kind=kOutput, calls=%fused_computation.14 | convolution fusion | flops 3224371200 | bytes 13107200 | tf_op jit(solution)/shard_map/tnk,tlk->tnl/dot_general | solution.py:135
  195.3 7.1 %fusion.38 = f32[2,256,256]{2,1,0:T(8,128)S(1)} fusion(f32[2,2048,256]{2,1,0:T(8,128)S(1)} %bitcast.52, f32[2,2048,256]{2,1,0:T(8,128)S(1)} %convolution_multiply_fusion), kind=kOutput, calls=%fused_computation.44 | convolution fusion | flops 3221225472 | bytes 8912896 | tf_op jit(solution)/shard_map/tnk,tnl->tkl/dot_general | solution.py:135
  202.4 7.1 %fusion.8 = f32[2,256,256]{2,1,0:T(8,128)S(1)} fusion(f32[2,2048,256]{2,1,0:T(8,128)S(1)} %convolution_multiply_fusion, f32[2,2048,256]{2,1,0:T(8,128)S(1)} %bitcast.46, f32[2,256]{1,0:T(2,128)S(1)} %compare_convert_fusion), kind=kOutput, calls=%fused_computation.10 | convolution fusion | flops 3222274048 | bytes 8914944 | tf_op jit(solution)/shard_map/tnk,tnl->tkl/dot_general | solution.py:135
  210.6 3.8 %fusion.14 = f32[2,256,2048]{1,2,0:T(8,128)S(1)} fusion(f32[2,256,256]{1,2,0:T(8,128)S(1)} %fusion.39, f32[2048,256]{1,0:T(8,128)S(1)} %copy-done.6), kind=kOutput, calls=%fused_computation.15 | convolution fusion | flops 3221225472 | bytes 6815744 | tf_op jit(solution)/shard_map/nk,tkl->tnl/dot_general | solution.py:135
  214.5 5.1 %fusion = f32[2,2048,256]{2,1,0:T(8,128)} fusion(f32[2,256,2048]{1,2,0:T(8,128)S(1)} %fusion.14, f32[2,256,256]{2,1,0:T(8,128)S(1)} %fusion.8, f32[2,2048,256]{2,1,0:T(8,128)S(1)} %bitcast.50, f32[2,256]{1,0:T(2,128)S(1)} %compare_convert_fusion), kind=kOutput, calls=%fused_computation.1 | convolution fusion | flops 3224371200 | bytes 13109248 | tf_op jit(solution)/shard_map/tnk,tkl->tnl/dot_general | solution.py:135
  (106 shorter events, 22.8 us)
Async XLA Ops:
  0.6 16.5 %collective-permute-start.4 = (bf16[64,2048]{1,0:T(8,128)(2,1)}, bf16[64,2048]{1,0:T(8,128)(2,1)}, u32[]{:S(2)}, u32[]{:S(2)}) collective-permute-start(bf16[64,2048]{1,0:T(8,128)(2,1)} %refs_2_), channel_id=1, source_target_pairs={{0,16},{8,24},{16,0},{24,8},{1,17},{9,25},{17,1},{25,9},{2,18},{10... | collective-permute-start | bytes 786440 | tf_op jit(solution)/shard_map/ppermute | solution.py:127
  4.7 22.6 %collective-permute-start.1 = (f32[512,256]{1,0:T(8,128)}, f32[512,256]{1,0:T(8,128)S(1)}, u32[]{:S(2)}, u32[]{:S(2)}) collective-permute-start(f32[512,256]{1,0:T(8,128)} %refs_6_), channel_id=1, source_target_pairs={{0,4},{1,5},{2,6},{3,7},{4,0},{5,1},{6,2},{7,3},{8,12},{9,13},{10,... | collective-permute-start | bytes 1572872 | tf_op jit(solution)/shard_map/ppermute | solution.py:127
  6.3 21.1 %collective-permute-start = (f32[512,256]{1,0:T(8,128)}, f32[512,256]{1,0:T(8,128)S(1)}, u32[]{:S(2)}, u32[]{:S(2)}) collective-permute-start(f32[512,256]{1,0:T(8,128)} %refs_6_), channel_id=1, source_target_pairs={{0,2},{1,3},{2,0},{3,1},{4,6},{5,7},{6,4},{7,5},{8,10},{9,11},{10,... | collective-permute-start | bytes 1572872 | tf_op jit(solution)/shard_map/ppermute | solution.py:127
  7.7 23.0 %collective-permute-start.2 = (f32[512,256]{1,0:T(8,128)}, f32[512,256]{1,0:T(8,128)S(1)}, u32[]{:S(2)}, u32[]{:S(2)}) collective-permute-start(f32[512,256]{1,0:T(8,128)} %refs_6_), channel_id=1, source_target_pairs={{0,6},{1,7},{2,4},{3,5},{4,2},{5,3},{6,0},{7,1},{8,14},{9,15},{10,... | collective-permute-start | bytes 1572872 | tf_op jit(solution)/shard_map/ppermute | solution.py:127
  8.2 14.4 %collective-permute-start.3 = (bf16[64,2048]{1,0:T(8,128)(2,1)}, bf16[64,2048]{1,0:T(8,128)(2,1)S(1)}, u32[]{:S(2)}, u32[]{:S(2)}) collective-permute-start(bf16[64,2048]{1,0:T(8,128)(2,1)} %refs_2_), channel_id=1, source_target_pairs={{0,8},{8,0},{16,24},{24,16},{1,9},{9,1},{17,25},{25,17},{2,10},{10... | collective-permute-start | bytes 786440 | tf_op jit(solution)/shard_map/ppermute | solution.py:127
  17.1 10.3 %collective-permute-start.5 = (bf16[64,2048]{1,0:T(8,128)(2,1)}, bf16[64,2048]{1,0:T(8,128)(2,1)S(1)}, u32[]{:S(2)}, u32[]{:S(2)}) collective-permute-start(bf16[64,2048]{1,0:T(8,128)(2,1)} %refs_2_), channel_id=1, source_target_pairs={{0,24},{8,16},{16,8},{24,0},{1,25},{9,17},{17,9},{25,1},{2,26},{10... | collective-permute-start | bytes 786440 | tf_op jit(solution)/shard_map/ppermute | solution.py:127
  30.7 2.8 %collective-permute-start.9 = (f32[512,256]{1,0:T(8,128)}, f32[512,256]{1,0:T(8,128)S(1)}, u32[]{:S(2)}, u32[]{:S(2)}) collective-permute-start(f32[512,256]{1,0:T(8,128)} %refs_6_), channel_id=1, source_target_pairs={{0,1},{1,0},{2,3},{3,2},{4,5},{5,4},{6,7},{7,6},{8,9},{9,8},{10,11... | collective-permute-start | bytes 1572872 | tf_op jit(solution)/shard_map/ppermute | solution.py:127
  30.7 4.1 %collective-permute-start.10 = (f32[512,256]{1,0:T(8,128)S(1)}, f32[512,256]{1,0:T(8,128)S(1)}, u32[]{:S(2)}, u32[]{:S(2)}) collective-permute-start(f32[512,256]{1,0:T(8,128)S(1)} %collective-permute-done.refs_7_), channel_id=1, source_target_pairs={{0,1},{1,0},{2,3},{3,2},{4,5},{5,4},{6,7},{7,6},{8,9},{9,8},{10,11... | collective-permute-start | bytes 1572872 | tf_op jit(solution)/shard_map/ppermute | solution.py:127
  31.3 6.2 %collective-permute-start.11 = (f32[512,256]{1,0:T(8,128)S(1)}, f32[512,256]{1,0:T(8,128)}, u32[]{:S(2)}, u32[]{:S(2)}) collective-permute-start(f32[512,256]{1,0:T(8,128)S(1)} %collective-permute-done.1.refs_8_), channel_id=1, source_target_pairs={{0,1},{1,0},{2,3},{3,2},{4,5},{5,4},{6,7},{7,6},{8,9},{9,8},{10,11... | collective-permute-start | bytes 1572872 | tf_op jit(solution)/shard_map/ppermute | solution.py:127
  31.3 6.2 %collective-permute-start.12 = (f32[512,256]{1,0:T(8,128)S(1)}, f32[512,256]{1,0:T(8,128)}, u32[]{:S(2)}, u32[]{:S(2)}) collective-permute-start(f32[512,256]{1,0:T(8,128)S(1)} %collective-permute-done.2.refs_9_), channel_id=1, source_target_pairs={{0,1},{1,0},{2,3},{3,2},{4,5},{5,4},{6,7},{7,6},{8,9},{9,8},{10,11... | collective-permute-start | bytes 1572872 | tf_op jit(solution)/shard_map/ppermute | solution.py:127
  31.8 14.3 %collective-permute-start.8 = (s32[392,256]{1,0:T(8,128)}, s32[392,256]{1,0:T(8,128)S(1)}, u32[]{:S(2)}, u32[]{:S(2)}) collective-permute-start(s32[392,256]{1,0:T(8,128)} %shard_map.95.refs_1_), channel_id=1, source_target_pairs={{0,24},{8,16},{16,8},{24,0},{1,25},{9,17},{17,9},{25,1},{2,26},{10... | collective-permute-start | bytes 1204232 | tf_op jit(solution)/shard_map/ppermute | solution.py:127
  33.6 46.1 %collective-permute-start.7 = (s32[392,256]{1,0:T(8,128)}, s32[392,256]{1,0:T(8,128)S(1)}, u32[]{:S(2)}, u32[]{:S(2)}) collective-permute-start(s32[392,256]{1,0:T(8,128)} %shard_map.95.refs_1_), channel_id=1, source_target_pairs={{0,16},{8,24},{16,0},{24,8},{1,17},{9,25},{17,1},{25,9},{2,18},{10... | collective-permute-start | bytes 1204232 | tf_op jit(solution)/shard_map/ppermute | solution.py:127
  34.8 44.9 %collective-permute-start.6 = (s32[392,256]{1,0:T(8,128)}, s32[392,256]{1,0:T(8,128)S(1)}, u32[]{:S(2)}, u32[]{:S(2)}) collective-permute-start(s32[392,256]{1,0:T(8,128)} %shard_map.95.refs_1_), channel_id=1, source_target_pairs={{0,8},{8,0},{16,24},{24,16},{1,9},{9,1},{17,25},{25,17},{2,10},{10... | collective-permute-start | bytes 1204232 | tf_op jit(solution)/shard_map/ppermute | solution.py:127
  43.6 55.4 %collective-permute-start.18 = (s32[200,512]{1,0:T(8,128)}, s32[200,512]{1,0:T(8,128)S(1)}, u32[]{:S(2)}, u32[]{:S(2)}) collective-permute-start(s32[200,512]{1,0:T(8,128)} %get-tuple-element.52), channel_id=1, source_target_pairs={{0,24},{8,16},{16,8},{24,0},{1,25},{9,17},{17,9},{25,1},{2,26},{10... | collective-permute-start | bytes 1228808 | tf_op jit(solution)/shard_map/ppermute | solution.py:127
  46.1 33.6 %copy-start.15 = (s32[392,256]{1,0:T(8,128)}, s32[392,256]{1,0:T(8,128)S(1)}, u32[]{:S(2)}) copy-start(s32[392,256]{1,0:T(8,128)S(1)} %collective-permute-done.8.refs_4_) | copy-start | bytes 1204228
  84.8 32.0 %collective-permute-start.13 = (s32[2,392,256]{2,1,0:T(8,128)}, s32[2,392,256]{2,1,0:T(8,128)S(1)}, u32[]{:S(2)}, u32[]{:S(2)}) collective-permute-start(s32[2,392,256]{2,1,0:T(8,128)} %get-tuple-element.58), channel_id=1, source_target_pairs={{0,2},{1,3},{2,0},{3,1},{4,6},{5,7},{6,4},{7,5},{8,10},{9,11},{10,... | collective-permute-start | bytes 2408456 | tf_op jit(solution)/shard_map/ppermute | solution.py:127
  86.3 35.3 %collective-permute-start.14 = (s32[2,392,256]{2,1,0:T(8,128)}, s32[2,392,256]{2,1,0:T(8,128)S(1)}, u32[]{:S(2)}, u32[]{:S(2)}) collective-permute-start(s32[2,392,256]{2,1,0:T(8,128)} %get-tuple-element.59), channel_id=1, source_target_pairs={{0,4},{1,5},{2,6},{3,7},{4,0},{5,1},{6,2},{7,3},{8,12},{9,13},{10,... | collective-permute-start | bytes 2408456 | tf_op jit(solution)/shard_map/ppermute | solution.py:127
  87.8 33.8 %collective-permute-start.15 = (s32[2,392,256]{2,1,0:T(8,128)}, s32[2,392,256]{2,1,0:T(8,128)S(1)}, u32[]{:S(2)}, u32[]{:S(2)}) collective-permute-start(s32[2,392,256]{2,1,0:T(8,128)} %get-tuple-element.60), channel_id=1, source_target_pairs={{0,6},{1,7},{2,4},{3,5},{4,2},{5,3},{6,0},{7,1},{8,14},{9,15},{10,... | collective-permute-start | bytes 2408456 | tf_op jit(solution)/shard_map/ppermute | solution.py:127
  98.9 17.6 %collective-permute-start.17 = (s32[200,512]{1,0:T(8,128)S(1)}, s32[200,512]{1,0:T(8,128)S(1)}, u32[]{:S(2)}, u32[]{:S(2)}) collective-permute-start(s32[200,512]{1,0:T(8,128)S(1)} %copy-done.25), channel_id=1, source_target_pairs={{0,16},{8,24},{16,0},{24,8},{1,17},{9,25},{17,1},{25,9},{2,18},{10... | collective-permute-start | bytes 1228808 | tf_op jit(solution)/shard_map/ppermute | solution.py:127
  99.0 17.8 %collective-permute-start.16 = (s32[200,512]{1,0:T(8,128)S(1)}, s32[200,512]{1,0:T(8,128)S(1)}, u32[]{:S(2)}, u32[]{:S(2)}) collective-permute-start(s32[200,512]{1,0:T(8,128)S(1)} %copy-done.25), channel_id=1, source_target_pairs={{0,8},{8,0},{16,24},{24,16},{1,9},{9,1},{17,25},{25,17},{2,10},{10... | collective-permute-start | bytes 1228808 | tf_op jit(solution)/shard_map/ppermute | solution.py:127
  105.4 23.1 %copy-start.7 = (s32[2,392,256]{2,1,0:T(8,128)S(1)}, s32[2,392,256]{2,1,0:T(8,128)}, u32[]{:S(2)}) copy-start(s32[2,392,256]{2,1,0:T(8,128)} %get-tuple-element.68.refs_1_) | copy-start | bytes 2408452
  116.7 20.9 %copy-start.8 = (s32[2,392,256]{2,1,0:T(8,128)}, s32[2,392,256]{2,1,0:T(8,128)S(1)}, u32[]{:S(2)}) copy-start(s32[2,392,256]{2,1,0:T(8,128)S(1)} %collective-permute-done.13.refs_2_) | copy-start | bytes 2408452
  121.6 16.1 %copy-start.9 = (s32[2,392,256]{2,1,0:T(8,128)}, s32[2,392,256]{2,1,0:T(8,128)S(1)}, u32[]{:S(2)}) copy-start(s32[2,392,256]{2,1,0:T(8,128)S(1)} %collective-permute-done.14.refs_3_) | copy-start | bytes 2408452
  121.6 16.1 %copy-start.10 = (s32[2,392,256]{2,1,0:T(8,128)}, s32[2,392,256]{2,1,0:T(8,128)S(1)}, u32[]{:S(2)}) copy-start(s32[2,392,256]{2,1,0:T(8,128)S(1)} %collective-permute-done.15.refs_4_) | copy-start | bytes 2408452
  128.3 6.6 %collective-permute-start.19 = (f32[4,512,256]{2,1,0:T(8,128)}, f32[4,512,256]{2,1,0:T(8,128)S(1)}, u32[]{:S(2)}, u32[]{:S(2)}) collective-permute-start(f32[4,512,256]{2,1,0:T(8,128)} %get-tuple-element.67), channel_id=1, source_target_pairs={{0,1},{1,0},{2,3},{3,2},{4,5},{5,4},{6,7},{7,6},{8,9},{9,8},{10,11... | collective-permute-start | bytes 6291464 | tf_op jit(solution)/shard_map/ppermute | solution.py:127
  128.4 10.8 %collective-permute-start.23 = (s32[2,392,256]{2,1,0:T(8,128)S(1)}, s32[2,392,256]{2,1,0:T(8,128)S(1)}, u32[]{:S(2)}, u32[]{:S(2)}) collective-permute-start(s32[2,392,256]{2,1,0:T(8,128)S(1)} %copy-done.7), channel_id=1, source_target_pairs={{0,1},{1,0},{2,3},{3,2},{4,5},{5,4},{6,7},{7,6},{8,9},{9,8},{10,11... | collective-permute-start | bytes 2408456 | tf_op jit(solution)/shard_map/ppermute | solution.py:127
  128.9 11.4 %collective-permute-start.24 = (s32[2,392,256]{2,1,0:T(8,128)S(1)}, s32[2,392,256]{2,1,0:T(8,128)S(1)}, u32[]{:S(2)}, u32[]{:S(2)}) collective-permute-start(s32[2,392,256]{2,1,0:T(8,128)S(1)} %collective-permute-done.13.refs_2_), channel_id=1, source_target_pairs={{0,1},{1,0},{2,3},{3,2},{4,5},{5,4},{6,7},{7,6},{8,9},{9,8},{10,11... | collective-permute-start | bytes 2408456 | tf_op jit(solution)/shard_map/ppermute | solution.py:127
  129.0 12.3 %collective-permute-start.25 = (s32[2,392,256]{2,1,0:T(8,128)S(1)}, s32[2,392,256]{2,1,0:T(8,128)S(1)}, u32[]{:S(2)}, u32[]{:S(2)}) collective-permute-start(s32[2,392,256]{2,1,0:T(8,128)S(1)} %collective-permute-done.14.refs_3_), channel_id=1, source_target_pairs={{0,1},{1,0},{2,3},{3,2},{4,5},{5,4},{6,7},{7,6},{8,9},{9,8},{10,11... | collective-permute-start | bytes 2408456 | tf_op jit(solution)/shard_map/ppermute | solution.py:127
  129.4 11.9 %collective-permute-start.26 = (s32[2,392,256]{2,1,0:T(8,128)S(1)}, s32[2,392,256]{2,1,0:T(8,128)S(1)}, u32[]{:S(2)}, u32[]{:S(2)}) collective-permute-start(s32[2,392,256]{2,1,0:T(8,128)S(1)} %collective-permute-done.15.refs_4_), channel_id=1, source_target_pairs={{0,1},{1,0},{2,3},{3,2},{4,5},{5,4},{6,7},{7,6},{8,9},{9,8},{10,11... | collective-permute-start | bytes 2408456 | tf_op jit(solution)/shard_map/ppermute | solution.py:127
  137.7 23.0 %collective-permute-start.22 = (f32[512,256]{1,0:T(8,128)}, f32[512,256]{1,0:T(8,128)}, u32[]{:S(2)}, u32[]{:S(2)}) collective-permute-start(f32[512,256]{1,0:T(8,128)} %get-tuple-element.84), channel_id=1, source_target_pairs={{0,6},{1,7},{2,4},{3,5},{4,2},{5,3},{6,0},{7,1},{8,14},{9,15},{10,... | collective-permute-start | bytes 1572872 | tf_op jit(solution)/shard_map/ppermute | solution.py:127
  139.2 24.8 %collective-permute-start.21 = (f32[512,256]{1,0:T(8,128)}, f32[512,256]{1,0:T(8,128)S(1)}, u32[]{:S(2)}, u32[]{:S(2)}) collective-permute-start(f32[512,256]{1,0:T(8,128)} %get-tuple-element.85), channel_id=1, source_target_pairs={{0,4},{1,5},{2,6},{3,7},{4,0},{5,1},{6,2},{7,3},{8,12},{9,13},{10,... | collective-permute-start | bytes 1572872 | tf_op jit(solution)/shard_map/ppermute | solution.py:127
  140.3 23.8 %collective-permute-start.20 = (f32[512,256]{1,0:T(8,128)}, f32[512,256]{1,0:T(8,128)S(1)}, u32[]{:S(2)}, u32[]{:S(2)}) collective-permute-start(f32[512,256]{1,0:T(8,128)} %get-tuple-element.86), channel_id=1, source_target_pairs={{0,2},{1,3},{2,0},{3,1},{4,6},{5,7},{6,4},{7,5},{8,10},{9,11},{10,... | collective-permute-start | bytes 1572872 | tf_op jit(solution)/shard_map/ppermute | solution.py:127
  (25 other events, 151.6 us)

commit v3 on v2

--- a/solution.py
+++ b/solution.py
@@ -102,29 +102,15 @@
                 work[t] = work[t][step:] - hot_dot(tail, solved, ((0,), (0,)))
 
 
-def factor_kernel(gram_ref, out_ref, scratch):
-    count, order, _ = gram_ref.shape
-
-    def put(t, lo, value):
-        out_ref[t, lo : lo + value.shape[0], :] = value
-
-    inverse_factor(lambda t: gram_ref[t], put, order, 64, scratch, count)
-
-
-def factor(gram, **kw):
-    return pl.pallas_call(
-        factor_kernel,
-        out_shape=jax.ShapeDtypeStruct(gram.shape, jnp.float32),
-        in_specs=[pl.BlockSpec(memory_space=pltpu.VMEM)],
-        out_specs=pl.BlockSpec(memory_space=pltpu.VMEM),
-        scratch_shapes=[pltpu.VMEM((gram.shape[0], SUB + 1, SUB, 128), jnp.float32)],
-        compiler_params=pltpu.CompilerParams(vmem_limit_bytes=32 * 1024 * 1024),
-        **kw,
-    )(gram)
-
-
 def flip(value, axis, size, mask):
     return lax.ppermute(value, axis, [(i, i ^ mask) for i in range(size)])
+
+
+def floor_gather(block, size):
+    got = {0: block}
+    for d in sorted(range(1, size), key=lambda d: (bin(d).count("1"), d)):
+        got[d] = flip(got[d & (d - 1)], "row", size, d & -d)
+    return [got[d] for d in range(size)]
 
 
 def after(value, *earlier):
@@ -182,6 +168,18 @@
     out_ref[3 * piece :, :] = jnp.broadcast_to(exponent, (8, width))
 
 
+def byte_planes(words):
+    piece = (words.shape[0] - 8) // 3
+    part = [words[piece * n : piece * (n + 1)] for n in range(3)]
+    planes = [
+        [p >> 24 for p in part] + [(part[2] << 24) >> 24],
+        [(p >> 16) & 255 for p in part] + [part[1] & 255],
+        [(p >> 8) & 255 for p in part] + [part[0] & 255],
+    ]
+    whole = [jnp.concatenate([x.astype(jnp.float32) for x in p], axis=0).astype(jnp.bfloat16) for p in planes]
+    return whole, power_of_two(words[3 * piece : 3 * piece + 1] - 23)
+
+
 def unpack(words):
     rows, width = words.shape
     piece = (rows - 8) // 3
@@ -200,8 +198,10 @@
         c.wait()
 
 
-def pack_kernel(value_ref, out_ref):
-    pack_into(value_ref[...], out_ref)
+def pack_kernel(right_ref, left_ref, both_ref, left_words_ref):
+    pack_into(right_ref[...], both_ref.at[0])
+    pack_into(left_ref[...], left_words_ref)
+    both_ref[1] = left_words_ref[...]
 
 
 def solve_kernel(rows, pairs, where_ref, rank_ref, *refs):
@@ -209,23 +209,27 @@
     out_ref, packed_ref, whole, right, sem = refs[rows + 2 * pairs :]
     floor, me = where_ref[0], where_ref[1]
     part = inverse[0].shape[0]
-    chunk, cap = held[0].shape
+    words, cap = held[0].shape[1:]
+    chunk = (words - 8) // 3 * 4
     quarters = pairs
     half, quarter = me // quarters, me % quarters
     moves = [
         (inverse[d], whole.at[pl.ds(pl.multiple_of((floor ^ d) * part, part), part), :]) for d in range(rows)
     ]
     for at in range(2 * pairs):
-        moves.append((held[at // 2] if at % 2 == 0 else other[at // 2], right.at[at]))
+        moves.append(((held if at % 2 == 0 else other)[at // 2].at[0], right.at[at]))
     load_all(moves, sem)
     column = lax.broadcasted_iota(jnp.int32, (1, cap), 1)
     for h in range(2):
         total = None
         for d in range(quarters):
             lhs = whole[:, pl.ds(pl.multiple_of((quarter ^ d) * chunk, chunk), chunk)]
-            for piece in split_three(right[h * quarters + d]):
-                term = jnp.dot(lhs, piece, preferred_element_type=jnp.float32)
-                total = term if total is None else total + term
+            planes, scale = byte_planes(right[h * quarters + d])
+            term = 0.0
+            for plane in planes:
+                term = term * 256.0 + jnp.dot(lhs, plane, preferred_element_type=jnp.float32)
+            term = term * scale
+            total = term if total is None else total + term
         tile = half ^ h
         kept = column < rank_ref[tile]
         out_ref[:, pl.ds(pl.multiple_of(tile * cap, cap), cap)] = jnp.where(kept, total, 0.0)
@@ -265,33 +269,165 @@
     ins, outs = refs[:rows], refs[rows:]
     mark = where_ref[0] ^ (where_ref[1] // 2)
     for e in range(pairs):
-        outs[e][0] = ins[0][...]
         for d in range(rows):
 
             @pl.when(mark == d ^ e)
             def _(d=d, e=e):
-                outs[e][1] = ins[d][...]
+                outs[e][...] = ins[d][...]
+
+
+def fold_kernel(pairs, mine_ref, theirs_ref, own_ref, *outs):
+    own_ref[...] = mine_ref[0] + theirs_ref[0]
+    for e in range(1, pairs):
+        pack_into(mine_ref[e] + theirs_ref[e], outs[e - 1])
 
 
 def spread_kernel(pairs, where_ref, *refs):
-    held, other, (row_ref, col_ref, words, sem) = refs[:pairs], refs[pairs : 2 * pairs], refs[2 * pairs :]
+    row_in, col_in = refs[: 2 * pairs], refs[2 * pairs : 4 * pairs]
+    row_ref, col_ref, col_pieces, words, sem = refs[4 * pairs :]
     me = where_ref[1]
     pair, side = me // 2, me % 2
     half = pairs // 2
-    load_all([(ref, words.at[n]) for n, ref in enumerate([*held, *other])], sem)
-
-    def put(ref, values, slot):
-        piece = values[0].shape[0]
+    moves = [(ref.at[1], words.at[n, 0]) for n, ref in enumerate(row_in)]
+    load_all(moves + [(ref, words.at[n, 1]) for n, ref in enumerate(col_in)], sem)
+
+    def put(values, slot, count, pieces, whole=None):
+        piece, cap = values[0].shape
         for i in range(4):
-            ref[pl.ds(pl.multiple_of(slot * (4 * piece) + piece * i, piece), piece), :] = values[i]
+            at = pl.ds(pl.multiple_of(slot * (4 * piece) + piece * i, piece), piece)
+            if whole is not None:
+                whole[at, :] = values[i]
+            for n, value in enumerate(split_three(values[i])[:count]):
+                pieces[at, n * cap : (n + 1) * cap] = value
 
     for n in range(2 * pairs):
-        put(row_ref, unpack(words[n, 0]), me ^ (2 * (n % pairs) + n // pairs))
+        put(unpack(words[n, 0]), me ^ (2 * (n % pairs) + n // pairs), 3, row_ref)
     upper = (pair // half) ^ side
     for n in range(pairs):
         e = n % half + half * upper
         from_other = n // half
-        put(col_ref, unpack(words[from_other * pairs + e, 1]), 2 * ((pair ^ e) % half) + (side ^ from_other))
+        slot = 2 * ((pair ^ e) % half) + (side ^ from_other)
+        put(unpack(words[from_other * pairs + e, 1]), slot, 2, col_pieces, col_ref)
+
+
+def stacked(pieces, picks):
+    return jnp.concatenate([pieces[n] for n in picks], axis=0)
+
+
+def wide_six(lhs, right):
+    cap = right.shape[0]
+    r = split_three(right)
+    total = jnp.dot(lhs, stacked(r, (0, 0, 0)), preferred_element_type=jnp.float32)
+    total += jnp.dot(lhs[:, : 2 * cap], stacked(r, (1, 1)), preferred_element_type=jnp.float32)
+    return total + jnp.dot(lhs[:, :cap], r[2], preferred_element_type=jnp.float32)
+
+
+def wide_three(lhs, right):
+    cap = right.shape[0]
+    r = split_three(right)
+    total = jnp.dot(lhs, stacked(r, (0, 0)), preferred_element_type=jnp.float32)
+    return total + jnp.dot(lhs[:, :cap], r[1], preferred_element_type=jnp.float32)
+
+
+def over_rows(x, y):
+    return lax.dot_general(x, y, (((0,), (0,)), ((), ())), preferred_element_type=jnp.float32)
+
+
+def local_kernel(rank_ref, left_ref, right_ref, probe_ref, part_ref, left_pieces, right_pieces):
+    tiles, order, cap = left_ref.shape
+    step = order // 4
+    row = lax.broadcasted_iota(jnp.int32, (cap, cap), 0)
+    column = lax.broadcasted_iota(jnp.int32, (cap, cap), 1)
+    for t in range(tiles):
+        product = jnp.zeros((cap, cap), jnp.float32)
+        for s in range(0, order, step):
+            product += hot_dot(right_ref[t, s : s + step], probe_ref[t, s : s + step], ((0,), (0,)))
+        rank = rank_ref[t, 0]
+        product = jnp.where((row < rank) & (column < rank), product, 0.0) / order
+        for s in range(0, order, step):
+            at = slice(s, s + step)
+            part_ref[t, at, :] = hot_dot(left_ref[t, at], product, ((1,), (0,)))
+            for ref, out in ((left_ref, left_pieces), (right_ref, right_pieces)):
+                for n, value in enumerate(split_three(ref[t, at])[:2]):
+                    out[t, at, n * cap : (n + 1) * cap] = value
+
+
+def final_kernel(parts, rank_ref, probe_ref, *refs):
+    cores = refs[:parts]
+    tall = refs[parts : parts + 5]
+    basis_out, factor_out = refs[parts + 5 : parts + 7]
+    part, panel, left, right, col, sampled, basis, outs, inverse, scratch, sem, sem_out = refs[parts + 7 :]
+    tiles, order, cap = part.shape
+    step = order // 4
+    loads = []
+    for t in range(tiles):
+        for src, dst in ((tall[0], part), (tall[1], panel)):
+            loads.append(pltpu.make_async_copy(src.at[t], dst.at[t], sem.at[len(loads)]))
+    for src, dst in ((tall[2], left), (tall[3], right), (tall[4], col)):
+        loads.append(pltpu.make_async_copy(src, dst, sem.at[len(loads)]))
+    for c in loads:
+        c.start()
+    root = math.sqrt(order)
+    row = lax.broadcasted_iota(jnp.int32, (cap, cap), 0)
+    column = lax.broadcasted_iota(jnp.int32, (cap, cap), 1)
+
+    total = cores[0][...]
+    for c in cores[1:]:
+        total = total + jnp.concatenate(unpack(c[...]), axis=0)
+
+    def core(t):
+        return total[t * cap : (t + 1) * cap] / order
+
+    grams = []
+    for t in range(tiles):
+        weight = hot_dot(core(t), probe_ref[t], ((1,), (0,))) / order
+        loads[2 * t].wait()
+        loads[2 * t + 1].wait()
+        same = jnp.zeros((cap, cap), jnp.float32)
+        cross = jnp.zeros((cap, cap), jnp.float32)
+        for s in range(0, order, step):
+            at = slice(s, s + step)
+            value = part[t, at] - wide_six(panel[t, at], weight)
+            pieces = split_three(value)
+            for n in range(3):
+                sampled[t, at, n * cap : (n + 1) * cap] = pieces[n]
+            product = over_rows(pieces[0], sampled[t, at])
+            same += product[:, :cap] + over_rows(pieces[1], pieces[1])
+            cross += product[:, cap : 2 * cap] + product[:, 2 * cap :]
+        gram = same + (cross + cross.T)
+        grams.append(gram + jnp.where((row == column) & (column >= rank_ref[t, 0]), 1.0, 0.0))
+
+    def put(t, lo, value):
+        inverse[t, lo : lo + value.shape[0], :] = value
+
+    inverse_factor(lambda t: grams[t], put, cap, 64, scratch, tiles)
+    for c in loads[2 * tiles :]:
+        c.wait()
+    sends = []
+    for t in range(tiles):
+        weight = inverse[t].T * root
+        left_proj = jnp.zeros((cap, cap), jnp.float32)
+        panel_proj = jnp.zeros((cap, cap), jnp.float32)
+        for s in range(0, order, step):
+            at = slice(s, s + step)
+            value = wide_six(sampled[t, at], weight)
+            outs[t, at, :] = value
+            high, low, _ = split_three(value)
+            one = over_rows(high, left[t, at])
+            left_proj += one[:, :cap] + one[:, cap:] + over_rows(low, left[t, at, :cap])
+            one = over_rows(high, panel[t, at, : 2 * cap])
+            panel_proj += one[:, :cap] + one[:, cap:] + over_rows(low, panel[t, at, :cap])
+        sends.append(pltpu.make_async_copy(outs.at[t], basis_out.at[t], sem_out.at[t]))
+        sends[-1].start()
+        left_proj = jnp.where(column < rank_ref[t, 0], left_proj, 0.0).T / order
+        core_proj = hot_dot(core(t), panel_proj, ((0,), (1,))) / order
+        for s in range(0, order, step):
+            at = slice(s, s + step)
+            basis[t, at, :] = wide_three(right[t, at], left_proj) - wide_three(col[at], core_proj)
+        sends.append(pltpu.make_async_copy(basis.at[t], factor_out.at[t], sem_out.at[tiles + t]))
+        sends[-1].start()
+    for c in sends:
+        c.wait()
 
 
 def make_shards(rows, cols):
@@ -303,7 +439,6 @@
         rank_cap = left.shape[1] // tile_cols
         chunk = panel_left.shape[0]
         part = factor_inverse.shape[0]
-        root_width = math.sqrt(tile_order)
         me = lax.axis_index("col").astype(jnp.int32)
         floor = lax.axis_index("row").astype(jnp.int32)
         spot = jnp.stack([floor, me])
@@ -311,12 +446,20 @@
         my_pair, my_side = me // 2, me % 2
         wide = tile_rows * rank_cap
 
-        words = call(pack_kernel, [shaped((packed_rows(chunk), rank_cap), jnp.int32)], [panel_left], "vv")[0]
-        inverse = [factor_inverse] + [flip(factor_inverse, "row", rows, d) for d in range(1, rows)]
-        held = [panel_right] + [flip(panel_right, "col", cols, 2 * e) for e in range(1, pairs)]
-        held, inverse, words = lax.optimization_barrier((held, inverse, words))
+        words_shape = (packed_rows(chunk), rank_cap)
+        both, words = call(
+            pack_kernel,
+            [shaped((2, *words_shape), jnp.int32), shaped(words_shape, jnp.int32)],
+            [panel_right, panel_left],
+            "vvvv",
+        )
+        inverse = floor_gather(factor_inverse, rows)
+        words = after(words, *inverse[1:])
+        held = [both] + [flip(both, "col", cols, 2 * e) for e in range(1, pairs)]
+        from_floors = floor_gather(words, rows)
+        first = [d for d in range(rows) if d & (d - 1) == 0]
+        held, inverse, _ = lax.optimization_barrier((held, inverse, [from_floors[d] for d in first]))
         other = [flip(h, "col", cols, 1) for h in held]
-        from_floors = [words] + [flip(words, "row", rows, d) for d in range(1, rows)]
 
         solved, solved_words = call(
             lambda *refs: solve_kernel(rows, pairs, *refs),
@@ -325,32 +468,31 @@
             "ss" + "a" * (rows + 2 * pairs) + "vv",
             [
                 pltpu.VMEM((rows * part, tile_order), jnp.bfloat16),
-                pltpu.VMEM((cols, chunk, rank_cap), jnp.float32),
+                pltpu.VMEM((cols, *words_shape), jnp.int32),
                 pltpu.SemaphoreType.DMA((rows + cols,)),
             ],
             flops=6 * rows * part * tile_order * wide,
         )
-        arrived = [flip(solved_words, "row", rows, d) for d in range(1, rows)]
+        arrived = floor_gather(solved_words, rows)[1:]
 
         *from_floors, _ = lax.optimization_barrier((*from_floors, solved_words))
         mixed = call(
             lambda *refs: choose_kernel(rows, pairs, *refs),
-            [shaped((2, *words.shape), jnp.int32)] * pairs,
+            [shaped(words_shape, jnp.int32)] * pairs,
             [spot, *from_floors],
             "s" + "v" * (rows + pairs),
         )
         mixed = [flip(mixed[e], "col", cols, 2 * e) if e else mixed[e] for e in range(pairs)]
 
-        kept_cols = (columns[None, :] < trail_rank).astype(jnp.float32)[:, None, :]
-
-        def to_tiles(block):
-            return block.reshape(tile_rows, tile_order, rank_cap) * kept_cols
-
-        tile_left = to_tiles(left)
-        tile_right = to_tiles(right)
-        tile_probe = to_tiles(probes)
-        right_probe = dot("tnk,tnl->tkl", tile_right, tile_probe)
-        tile_part = dot("tnk,tkl->tnl", tile_left, right_probe)
+        tall = (tile_rows, tile_order, rank_cap)
+        pieces = lambda n: shaped((tile_rows, tile_order, n * rank_cap), jnp.bfloat16)
+        tile_part, left_pieces, right_pieces = call(
+            local_kernel,
+            [shaped(tall), pieces(2), pieces(2)],
+            [trail_rank, left.reshape(tall), right.reshape(tall), probes.reshape(tall)],
+            "svvvvvv",
+            flops=24 * tile_rows * tile_order * rank_cap * rank_cap,
+        )
         mixed, arrived, tile_part = lax.optimization_barrier((mixed, arrived, tile_part))
         swapped = [flip(m, "col", cols, 1) for m in mixed]
 
@@ -366,34 +508,59 @@
             flops=6 * rows * part * wide * wide * pairs,
         )
         theirs = flip(theirs, "col", cols, 1)
-        parts = [mine[e] + theirs[e] for e in range(pairs)]
+        parts = call(
+            lambda *refs: fold_kernel(pairs, *refs),
+            [shaped((wide, rank_cap))] + [shaped((packed_rows(wide), rank_cap), jnp.int32)] * (pairs - 1),
+            [mine, theirs],
+            "vv" + "v" * pairs,
+        )
         swapped = lax.optimization_barrier((swapped, parts))[0]
         parts = [flip(parts[e], "col", cols, 2 * e) if e else parts[e] for e in range(pairs)]
-        row_left, col_left = call(
+        panel_pieces, col_left, col_pieces = call(
             lambda *refs: spread_kernel(pairs, *refs),
-            [shaped((cols * chunk, rank_cap)), shaped((pairs * chunk, rank_cap))],
-            [spot, *mixed, *swapped],
-            "s" + "a" * (2 * pairs) + "vv",
-            [pltpu.VMEM((2 * pairs, 2, *words.shape), jnp.int32), pltpu.SemaphoreType.DMA((2 * pairs,))],
-        )
-        row_left = row_left.reshape(tile_rows, tile_order, rank_cap)
-
-        panel_probe = dot("nk,tnl->tkl", col_left, tile_probe)
-        parts, panel_probe, row_left = lax.optimization_barrier((parts, panel_probe, row_left))
-        panel_core = sum(parts).reshape(tile_rows, rank_cap, rank_cap) / tile_order
-        core_probe = dot("tkl,tlm->tkm", panel_core, panel_probe)
-        sampled = (tile_part - dot("tnk,tkl->tnl", row_left, core_probe)) / tile_order
-        identity = (columns[:, None] == columns[None, :]).astype(jnp.float32)
-        gram_matrix = dot("tnk,tnl->tkl", sampled, sampled)
-        gram_matrix = gram_matrix + (1.0 - kept_cols) * identity
-        inverse_gram = factor(gram_matrix)
-        new_basis = dot("tnk,tlk->tnl", sampled, inverse_gram) * root_width
-        left_proj = dot("tnk,tnl->tkl", tile_left, new_basis)
-        panel_proj = dot("tnk,tnl->tkl", row_left, new_basis)
-        core_proj = dot("tlk,tlm->tkm", panel_core, panel_proj)
-        new_factor = (
-            dot("tnk,tkl->tnl", tile_right, left_proj) - dot("nk,tkl->tnl", col_left, core_proj)
-        ) / tile_order
+            [
+                shaped((cols * chunk, 3 * rank_cap), jnp.bfloat16),
+                shaped((pairs * chunk, rank_cap)),
+                shaped((pairs * chunk, 2 * rank_cap), jnp.bfloat16),
+            ],
+            [spot, *held, *other, *mixed, *swapped],
+            "s" + "a" * (4 * pairs) + "vvv",
+            [pltpu.VMEM((2 * pairs, 2, *words_shape), jnp.int32), pltpu.SemaphoreType.DMA((4 * pairs,))],
+        )
+        panel_probe = dot("nk,tnl->tkl", col_left, probes.reshape(tall))
+        panel_probe = jnp.where(columns[None, None, :] < trail_rank[:, :, None], panel_probe, 0.0)
+        parts, panel_probe, panel_pieces = lax.optimization_barrier((parts, panel_probe, panel_pieces))
+
+        new_basis, new_factor = call(
+            lambda *refs: final_kernel(pairs, *refs),
+            [shaped(tall), shaped(tall)],
+            [
+                trail_rank,
+                panel_probe,
+                *parts,
+                tile_part,
+                panel_pieces.reshape(tile_rows, tile_order, 3 * rank_cap),
+                left_pieces,
+                right_pieces,
+                col_pieces,
+            ],
+            "sv" + "v" * pairs + "aaaaa" + "aa",
+            [
+                pltpu.VMEM(tall, jnp.float32),
+                pltpu.VMEM((tile_rows, tile_order, 3 * rank_cap), jnp.bfloat16),
+                pltpu.VMEM((tile_rows, tile_order, 2 * rank_cap), jnp.bfloat16),
+                pltpu.VMEM((tile_rows, tile_order, 2 * rank_cap), jnp.bfloat16),
+                pltpu.VMEM((tile_order, 2 * rank_cap), jnp.bfloat16),
+                pltpu.VMEM((tile_rows, tile_order, 3 * rank_cap), jnp.bfloat16),
+                pltpu.VMEM(tall, jnp.float32),
+                pltpu.VMEM(tall, jnp.float32),
+                pltpu.VMEM((tile_rows, rank_cap, rank_cap), jnp.float32),
+                pltpu.VMEM((tile_rows, SUB + 1, SUB, 128), jnp.float32),
+                pltpu.SemaphoreType.DMA((2 * tile_rows + 3,)),
+                pltpu.SemaphoreType.DMA((2 * tile_rows,)),
+            ],
+            flops=60 * tile_rows * tile_order * rank_cap * rank_cap,
+        )
         return (
             new_basis.reshape(tile_rows * tile_order, rank_cap),
             new_factor.reshape(tile_rows * tile_order, rank_cap),

time: 224 us -> 194 us (0.87)
  matrix products: 66.4 us -> 7.27 us
  Pallas kernels: 38.9 us -> 91.4 us
  waiting for transfers between devices: 75.2 us -> 59.9 us
  other arithmetic: 5.31 us -> 0.74 us
  starting transfers between devices: 29.2 us -> 25.1 us
    pallas_call x5 -> x8, Pallas kernels: 25.8 us -> 91.4 us  [call(): pl.pallas_call(kernel, out_shape=out, in_specs=[pl.BlockSpec(memory_space...]
    dot_general x12 -> x1, matrix products: 66.4 us -> 7.27 us  [dot(): jnp.einsum(spec, a, b, precision=highest, preferred_element_type=jnp.floa...]
    ppermute x27, waiting for transfers between devices: 75.2 us -> 59.9 us  [flip(): return lax.ppermute(value, axis, [(i, i ^ mask) for i in range(size)])]
    pallas_call x1 -> x0, Pallas kernels: 13.1 us -> none  [factor(): pl.pallas_call(factor_kernel, out_shape=jax.ShapeDtypeStruct(gram.shape,...]
    ppermute x27, starting transfers between devices: 29.2 us -> 25.1 us  [flip(): return lax.ppermute(value, axis, [(i, i ^ mask) for i in range(size)])]
    add x1 -> x0, other arithmetic: 2.76 us -> none  [shards(): parts = [mine[e] + theirs[e] for e in range(pairs)]]
    unnamed x60 -> x45, local copies, waits for them, and re-layouts: 3.5 us -> 4.74 us
  transfers between devices with their start and end apart: 27 -> 27, of which waited for: 12 -> 12; matrix products, arithmetic and copies ran while one was open for 13% -> 5% of each run, Pallas kernels for 9% -> 21%
where the time goes in v3:
time: 194 us; the launch traced here: 190 us
  Pallas kernels  91.4 us (47%)
  waiting for transfers between devices  59.9 us (31%)
  starting transfers between devices  25.1 us (13%)
  matrix products  7.27 us (4%)
  local copies, waits for them, and re-layouts  4.74 us (2%)
    pallas_call x8, Pallas kernels, call(): pl.pallas_call(kernel, out_shape=out, in_specs=[pl.BlockSpec(memory_space...  91.4 us
    ppermute x27, waiting for transfers between devices, flip(): return lax.ppermute(value, axis, [(i, i ^ mask) for i in range(size)])  59.9 us
    ppermute x27, starting transfers between devices, flip(): return lax.ppermute(value, axis, [(i, i ^ mask) for i in range(size)])  25.1 us
    dot_general x1, matrix products, dot(): jnp.einsum(spec, a, b, precision=highest, preferred_element_type=jnp.floa...  7.27 us
    unnamed x45, local copies, waits for them, and re-layouts  4.74 us
  transfers between devices with their start and end apart: 27, of which 12 were waited for; matrix products, arithmetic and copies ran while one was open for 5% of the time, Pallas kernels for 21%

profile of v3, /device:TPU:0, one launch (start us, length us, event | category | flops | bytes accessed | tf_op | source)
XLA Modules:
  0.0 190.4 jit_solution(18313468952176002212)
XLA Ops:
  0.6 4.1 %collective-permute-start.4 = (bf16[64,2048]{1,0:T(8,128)(2,1)}, bf16[64,2048]{1,0:T(8,128)(2,1)S(1)}, u32[]{:S(2)}, u32[]{:S(2)}) collective-permute-start(bf16[64,2048]{1,0:T(8,128)(2,1)} %refs_2_), channel_id=1, source_target_pairs={{0,16},{8,24},{16,0},{24,8},{1,17},{9,25},{17,1},{25,9},{2,18},{10... | collective-permute-start | bytes 786440 | tf_op jit(solution)/shard_map/ppermute | solution.py:106
  4.7 2.5 %shard_map.95 = (s32[2,392,256]{2,1,0:T(8,128)}, s32[392,256]{1,0:T(8,128)}) custom-call(f32[512,256]{1,0:T(8,128)} %right_ref.1, f32[512,256]{1,0:T(8,128)} %left_ref.1), custom_call_target="tpu_custom_call" | custom-call | bytes 2252800 | tf_op jit(solution)/shard_map/pallas_call | solution.py:131
  7.2 1.5 collective-permute-start
  8.7 1.5 collective-permute-start.1
  10.7 1.6 collective-permute-start.3
  12.3 4.7 %collective-permute-done.4.refs_4_ = bf16[64,2048]{1,0:T(8,128)(2,1)S(1)} collective-permute-done((bf16[64,2048]{1,0:T(8,128)(2,1)}, bf16[64,2048]{1,0:T(8,128)(2,1)S(1)}, u32[]{:S(2)}, u32[]{:S(2)}) %collective-permute-start.4) | collective-permute-done | bytes 262176 | tf_op jit(solution)/shard_map/ppermute | solution.py:106
  17.0 0.8 collective-permute-start.5
  17.8 4.9 %collective-permute-done.3.refs_3_ = bf16[64,2048]{1,0:T(8,128)(2,1)S(1)} collective-permute-done((bf16[64,2048]{1,0:T(8,128)(2,1)}, bf16[64,2048]{1,0:T(8,128)(2,1)S(1)}, u32[]{:S(2)}, u32[]{:S(2)}) %collective-permute-start.3) | collective-permute-done | bytes 262176 | tf_op jit(solution)/shard_map/ppermute | solution.py:106
  22.7 5.2 %collective-permute-done.5.refs_5_ = bf16[64,2048]{1,0:T(8,128)(2,1)S(1)} collective-permute-done((bf16[64,2048]{1,0:T(8,128)(2,1)S(1)}, bf16[64,2048]{1,0:T(8,128)(2,1)S(1)}, u32[]{:S(2)}, u32[]{:S(2)}) %collective-permute-start.5) | collective-permute-done | bytes 262176 | tf_op jit(solution)/shard_map/ppermute | solution.py:106
  28.4 2.5 %collective-permute-start.6 = (s32[392,256]{1,0:T(8,128)}, s32[392,256]{1,0:T(8,128)S(1)}, u32[]{:S(2)}, u32[]{:S(2)}) collective-permute-start(s32[392,256]{1,0:T(8,128)} %get-tuple-element.68.refs_1_), channel_id=1, source_target_pairs={{0,8},{8,0},{16,24},{24,16},{1,9},{9,1},{17,25},{25,17},{2,10},{10... | collective-permute-start | bytes 1204232 | tf_op jit(solution)/shard_map/ppermute | solution.py:106
  30.9 14.3 %collective-permute-done.1.refs_8_.refs_3_ = s32[2,392,256]{2,1,0:T(8,128)S(1)} collective-permute-done((s32[2,392,256]{2,1,0:T(8,128)}, s32[2,392,256]{2,1,0:T(8,128)S(1)}, u32[]{:S(2)}, u32[]{:S(2)}) %collective-permute-start.1) | collective-permute-done | bytes 802848 | tf_op jit(solution)/shard_map/ppermute | solution.py:106
  45.2 2.5 %collective-permute-done.7.refs_3_ = s32[392,256]{1,0:T(8,128)} collective-permute-done((s32[392,256]{1,0:T(8,128)}, s32[392,256]{1,0:T(8,128)}, u32[]{:S(2)}, u32[]{:S(2)}) %collective-permute-start.7) | collective-permute-done | bytes 401440 | tf_op jit(solution)/shard_map/ppermute | solution.py:106
  49.6 0.8 collective-permute-done.10.refs_12_.refs_7_
  50.4 1.7 collective-permute-done.11.refs_13_.refs_8_
  52.1 0.9 collective-permute-done.8.refs_10_.refs_5_
  53.7 5.9 %shard_map.96 = (f32[256,512]{1,0:T(8,128)}, s32[200,512]{1,0:T(8,128)}) custom-call(s32[2]{0:T(128)} %pad_add_fusion.refs_0_, s32[2]{0:T(128)} %refs_1_.1, bf16[64,2048]{1,0:T(8,128)(2,1)} %refs_2_, bf16[64,2048]{1,0:T(8,128)(2,1)} %copy-done.13, bf16[64,2048]{1,0:T(8,128)(2,1)} %copy-done.12, bf16[64,2048]{1,0:T(8,128)(2,1)} %copy-done.14, ...), custom_call_target="tpu_custom_call" | custom-call | flops 1610612736 | bytes 8405008 | tf_op jit(solution)/shard_map/pallas_call | solution.py:131
  60.3 2.2 %collective-permute-start.12 = (s32[392,256]{1,0:T(8,128)}, s32[392,256]{1,0:T(8,128)S(1)}, u32[]{:S(2)}, u32[]{:S(2)}) collective-permute-start(s32[392,256]{1,0:T(8,128)} %collective-permute-done.7.refs_3_), channel_id=1, source_target_pairs={{0,8},{8,0},{16,24},{24,16},{1,9},{9,1},{17,25},{25,17},{2,10},{10... | collective-permute-start | bytes 1204232 | tf_op jit(solution)/shard_map/ppermute | solution.py:106
  63.1 18.3 %collective-permute-done.12.refs_4_ = s32[392,256]{1,0:T(8,128)S(1)} collective-permute-done((s32[392,256]{1,0:T(8,128)}, s32[392,256]{1,0:T(8,128)S(1)}, u32[]{:S(2)}, u32[]{:S(2)}) %collective-permute-start.12) | collective-permute-done | bytes 401440 | tf_op jit(solution)/shard_map/ppermute | solution.py:106
  81.4 0.8 copy-done.11
  82.2 3.2 %shard_map.97 = (s32[392,256]{1,0:T(8,128)}, s32[392,256]{1,0:T(8,128)}, s32[392,256]{1,0:T(8,128)}, s32[392,256]{1,0:T(8,128)}) custom-call(s32[2]{0:T(128)} %pad_add_fusion.refs_0_, s32[392,256]{1,0:T(8,128)} %get-tuple-element.68.refs_1_, s32[392,256]{1,0:T(8,128)} %copy-done.10, s32[392,256]{1,0:T(8,128)} %collective-permute-done.7.refs_3_, ...), custom_call_target="tpu_custom_call" | custom-call | bytes 3211272 | tf_op jit(solution)/shard_map/pallas_call | solution.py:131
  85.4 1.6 collective-permute-start.13
  87.0 1.5 collective-permute-start.14
  88.9 19.7 %shard_map.98 = (f32[2,2048,256]{2,1,0:T(8,128)}, bf16[2,2048,512]{2,1,0:T(8,128)(2,1)}, bf16[2,2048,512]{2,1,0:T(8,128)(2,1)}) custom-call(s32[2,1]{1,0:T(2,128)} %copy.12.rank_ref.refs_0_, f32[2,2048,256]{2,1,0:T(8,128)} %bitcast.22, f32[2,2048,256]{2,1,0:T(8,128)} %bitcast.23, f32[2,2048,256]{2,1,0:T(8,128)} %bitcast.19), custom_call_target="tpu_custom_call" | custom-call | flops 6442450944 | bytes 25165832 | tf_op jit(solution)/shard_map/pallas_call | solution.py:131
  109.5 6.5 %shard_map.99 = (f32[4,512,256]{2,1,0:T(8,128)}, f32[4,512,256]{2,1,0:T(8,128)}) custom-call(s32[2]{0:T(128)} %pad_add_fusion.refs_0_, f32[256,512]{1,0:T(8,128)} %get-tuple-element.66.refs_1_, s32[200,512]{1,0:T(8,128)} %copy-done.16, s32[200,512]{1,0:T(8,128)} %copy-done.15, s32[200,512]{1,0:T(8,128)} %copy-done.17), custom_call_target="tpu_custom_call" | custom-call | flops 1610612736 | bytes 5947400 | tf_op jit(solution)/shard_map/pallas_call | solution.py:131
  117.1 5.4 %collective-permute-done.19.refs_1_ = f32[4,512,256]{2,1,0:T(8,128)S(1)} collective-permute-done((f32[4,512,256]{2,1,0:T(8,128)}, f32[4,512,256]{2,1,0:T(8,128)S(1)}, u32[]{:S(2)}, u32[]{:S(2)}) %collective-permute-start.19) | collective-permute-done | bytes 2097184 | tf_op jit(solution)/shard_map/ppermute | solution.py:106
  122.5 1.3 copy-done.4
  123.8 3.7 %shard_map.100 = (f32[512,256]{1,0:T(8,128)}, s32[392,256]{1,0:T(8,128)}, s32[392,256]{1,0:T(8,128)}, s32[392,256]{1,0:T(8,128)}) custom-call(f32[4,512,256]{2,1,0:T(8,128)} %get-tuple-element.80.refs_0_, f32[4,512,256]{2,1,0:T(8,128)} %copy-done.4), custom_call_target="tpu_custom_call" | custom-call | bytes 5922816 | tf_op jit(solution)/shard_map/pallas_call | solution.py:131
  127.5 1.7 collective-permute-start.20
  129.3 1.5 collective-permute-start.21
  131.2 10.1 %shard_map.101 = (bf16[4096,768]{1,0:T(8,128)(2,1)}, f32[2048,256]{1,0:T(8,128)}, bf16[2048,512]{1,0:T(8,128)(2,1)}) custom-call(s32[2]{0:T(128)} %pad_add_fusion.refs_0_, s32[2,392,256]{2,1,0:T(8,128)} %get-tuple-element.62.refs_6_.refs_1_, s32[2,392,256]{2,1,0:T(8,128)} %copy-done, s32[2,392,256]{2,1,0:T(8,128)} %copy-done.1, s32[2,392,256]{2,1,0:T(8,128)} %copy-done.2, ...), custom_call_target="tpu_custom_call" | custom-call | bytes 20119560 | tf_op jit(solution)/shard_map/pallas_call | solution.py:131
  141.3 7.3 %fusion.5.refs_1_ = f32[2,256,256]{2,1,0:T(8,128)} fusion(f32[2,2048,256]{2,1,0:T(8,128)} %bitcast.20, f32[2048,256]{1,0:T(8,128)} %get-tuple-element.94, pred[2,256]{1,0:T(4,128)(4,1)S(1)} %iota_compare_fusion), kind=kOutput, calls=%fused_computation.3 | convolution fusion | flops 3221356544 | bytes 6816256 | tf_op jit(solution)/shard_map/nk,tnl->tkl/dot_general | solution.py:121
  150.0 39.9 %shard_map.102 = (f32[2,2048,256]{2,1,0:T(8,128)}, f32[2,2048,256]{2,1,0:T(8,128)}) custom-call(s32[2,1]{1,0:T(2,128)} %copy.12.rank_ref.refs_0_, f32[2,256,256]{2,1,0:T(8,128)} %fusion.5.refs_1_, f32[512,256]{1,0:T(8,128)} %get-tuple-element.97.refs_2_, s32[392,256]{1,0:T(8,128)} %copy-done.18, s32[392,256]{1,0:T(8,128)} %copy-done.19, ...), custom_call_target="tpu_custom_call" | custom-call | flops 16106127360 | bytes 31612936 | tf_op jit(solution)/shard_map/pallas_call | solution.py:131
  (78 shorter events, 9.1 us)
Async XLA Ops:
  0.6 61.8 %copy-start.21 = (s32[2,1]{0,1:T(1,128)S(1)}, s32[2,1]{0,1:T(1,128)}, u32[]{:S(2)}) copy-start(s32[2,1]{0,1:T(1,128)} %param.15) | copy-start | bytes 28
  0.6 16.3 %collective-permute-start.4 = (bf16[64,2048]{1,0:T(8,128)(2,1)}, bf16[64,2048]{1,0:T(8,128)(2,1)S(1)}, u32[]{:S(2)}, u32[]{:S(2)}) collective-permute-start(bf16[64,2048]{1,0:T(8,128)(2,1)} %refs_2_), channel_id=1, source_target_pairs={{0,16},{8,24},{16,0},{24,8},{1,17},{9,25},{17,1},{25,9},{2,18},{10... | collective-permute-start | bytes 786440 | tf_op jit(solution)/shard_map/ppermute | solution.py:106
  7.2 23.7 %collective-permute-start = (s32[2,392,256]{2,1,0:T(8,128)}, s32[2,392,256]{2,1,0:T(8,128)S(1)}, u32[]{:S(2)}, u32[]{:S(2)}) collective-permute-start(s32[2,392,256]{2,1,0:T(8,128)} %get-tuple-element.62.refs_6_.refs_1_), channel_id=1, source_target_pairs={{0,2},{1,3},{2,0},{3,1},{4,6},{5,7},{6,4},{7,5},{8,10},{9,11},{10,... | collective-permute-start | bytes 2408456 | tf_op jit(solution)/shard_map/ppermute | solution.py:106
  8.7 36.5 %collective-permute-start.1 = (s32[2,392,256]{2,1,0:T(8,128)}, s32[2,392,256]{2,1,0:T(8,128)S(1)}, u32[]{:S(2)}, u32[]{:S(2)}) collective-permute-start(s32[2,392,256]{2,1,0:T(8,128)} %get-tuple-element.62.refs_6_.refs_1_), channel_id=1, source_target_pairs={{0,4},{1,5},{2,6},{3,7},{4,0},{5,1},{6,2},{7,3},{8,12},{9,13},{10,... | collective-permute-start | bytes 2408456 | tf_op jit(solution)/shard_map/ppermute | solution.py:106
  10.2 35.0 %collective-permute-start.2 = (s32[2,392,256]{2,1,0:T(8,128)}, s32[2,392,256]{2,1,0:T(8,128)S(1)}, u32[]{:S(2)}, u32[]{:S(2)}) collective-permute-start(s32[2,392,256]{2,1,0:T(8,128)} %get-tuple-element.62.refs_6_.refs_1_), channel_id=1, source_target_pairs={{0,6},{1,7},{2,4},{3,5},{4,2},{5,3},{6,0},{7,1},{8,14},{9,15},{10,... | collective-permute-start | bytes 2408456 | tf_op jit(solution)/shard_map/ppermute | solution.py:106
  10.7 12.0 %collective-permute-start.3 = (bf16[64,2048]{1,0:T(8,128)(2,1)}, bf16[64,2048]{1,0:T(8,128)(2,1)S(1)}, u32[]{:S(2)}, u32[]{:S(2)}) collective-permute-start(bf16[64,2048]{1,0:T(8,128)(2,1)} %refs_2_), channel_id=1, source_target_pairs={{0,8},{8,0},{16,24},{24,16},{1,9},{9,1},{17,25},{25,17},{2,10},{10... | collective-permute-start | bytes 786440 | tf_op jit(solution)/shard_map/ppermute | solution.py:106
  17.0 36.6 %copy-start.12 = (bf16[64,2048]{1,0:T(8,128)(2,1)}, bf16[64,2048]{1,0:T(8,128)(2,1)S(1)}, u32[]{:S(2)}) copy-start(bf16[64,2048]{1,0:T(8,128)(2,1)S(1)} %collective-permute-done.4.refs_4_) | copy-start | bytes 786436
  17.0 10.9 %collective-permute-start.5 = (bf16[64,2048]{1,0:T(8,128)(2,1)S(1)}, bf16[64,2048]{1,0:T(8,128)(2,1)S(1)}, u32[]{:S(2)}, u32[]{:S(2)}) collective-permute-start(bf16[64,2048]{1,0:T(8,128)(2,1)S(1)} %collective-permute-done.4.refs_4_), channel_id=1, source_target_pairs={{0,8},{8,0},{16,24},{24,16},{1,9},{9,1},{17,25},{25,17},{2,10},{10... | collective-permute-start | bytes 786440 | tf_op jit(solution)/shard_map/ppermute | solution.py:106
  22.7 25.0 %copy-start.13 = (bf16[64,2048]{1,0:T(8,128)(2,1)}, bf16[64,2048]{1,0:T(8,128)(2,1)S(1)}, u32[]{:S(2)}) copy-start(bf16[64,2048]{1,0:T(8,128)(2,1)S(1)} %collective-permute-done.3.refs_3_) | copy-start | bytes 786436
  27.9 19.8 %copy-start.14 = (bf16[64,2048]{1,0:T(8,128)(2,1)}, bf16[64,2048]{1,0:T(8,128)(2,1)S(1)}, u32[]{:S(2)}) copy-start(bf16[64,2048]{1,0:T(8,128)(2,1)S(1)} %collective-permute-done.5.refs_5_) | copy-start | bytes 786436
  27.9 19.8 %collective-permute-start.7 = (s32[392,256]{1,0:T(8,128)}, s32[392,256]{1,0:T(8,128)}, u32[]{:S(2)}, u32[]{:S(2)}) collective-permute-start(s32[392,256]{1,0:T(8,128)} %get-tuple-element.68.refs_1_), channel_id=1, source_target_pairs={{0,16},{8,24},{16,0},{24,8},{1,17},{9,25},{17,1},{25,9},{2,18},{10... | collective-permute-start | bytes 1204232 | tf_op jit(solution)/shard_map/ppermute | solution.py:106
  28.4 19.3 %collective-permute-start.6 = (s32[392,256]{1,0:T(8,128)}, s32[392,256]{1,0:T(8,128)S(1)}, u32[]{:S(2)}, u32[]{:S(2)}) collective-permute-start(s32[392,256]{1,0:T(8,128)} %get-tuple-element.68.refs_1_), channel_id=1, source_target_pairs={{0,8},{8,0},{16,24},{24,16},{1,9},{9,1},{17,25},{25,17},{2,10},{10... | collective-permute-start | bytes 1204232 | tf_op jit(solution)/shard_map/ppermute | solution.py:106
  30.9 22.7 %copy-start = (s32[2,392,256]{2,1,0:T(8,128)}, s32[2,392,256]{2,1,0:T(8,128)S(1)}, u32[]{:S(2)}) copy-start(s32[2,392,256]{2,1,0:T(8,128)S(1)} %collective-permute-done.refs_7_.refs_2_) | copy-start | bytes 2408452
  47.7 2.7 %collective-permute-start.10 = (s32[2,392,256]{2,1,0:T(8,128)S(1)}, s32[2,392,256]{2,1,0:T(8,128)S(1)}, u32[]{:S(2)}, u32[]{:S(2)}) collective-permute-start(s32[2,392,256]{2,1,0:T(8,128)S(1)} %collective-permute-done.1.refs_8_.refs_3_), channel_id=1, source_target_pairs={{0,1},{1,0},{2,3},{3,2},{4,5},{5,4},{6,7},{7,6},{8,9},{9,8},{10,11... | collective-permute-start | bytes 2408456 | tf_op jit(solution)/shard_map/ppermute | solution.py:106
  47.8 4.4 %collective-permute-start.11 = (s32[2,392,256]{2,1,0:T(8,128)S(1)}, s32[2,392,256]{2,1,0:T(8,128)}, u32[]{:S(2)}, u32[]{:S(2)}) collective-permute-start(s32[2,392,256]{2,1,0:T(8,128)S(1)} %collective-permute-done.2.refs_9_.refs_4_), channel_id=1, source_target_pairs={{0,1},{1,0},{2,3},{3,2},{4,5},{5,4},{6,7},{7,6},{8,9},{9,8},{10,11... | collective-permute-start | bytes 2408456 | tf_op jit(solution)/shard_map/ppermute | solution.py:106
  48.4 4.6 %collective-permute-start.8 = (s32[2,392,256]{2,1,0:T(8,128)}, s32[2,392,256]{2,1,0:T(8,128)}, u32[]{:S(2)}, u32[]{:S(2)}) collective-permute-start(s32[2,392,256]{2,1,0:T(8,128)} %get-tuple-element.62.refs_6_.refs_1_), channel_id=1, source_target_pairs={{0,1},{1,0},{2,3},{3,2},{4,5},{5,4},{6,7},{7,6},{8,9},{9,8},{10,11... | collective-permute-start | bytes 2408456 | tf_op jit(solution)/shard_map/ppermute | solution.py:106
  48.4 5.2 %collective-permute-start.9 = (s32[2,392,256]{2,1,0:T(8,128)S(1)}, s32[2,392,256]{2,1,0:T(8,128)}, u32[]{:S(2)}, u32[]{:S(2)}) collective-permute-start(s32[2,392,256]{2,1,0:T(8,128)S(1)} %collective-permute-done.refs_7_.refs_2_), channel_id=1, source_target_pairs={{0,1},{1,0},{2,3},{3,2},{4,5},{5,4},{6,7},{7,6},{8,9},{9,8},{10,11... | collective-permute-start | bytes 2408456 | tf_op jit(solution)/shard_map/ppermute | solution.py:106
  59.6 29.3 %collective-permute-start.17 = (s32[200,512]{1,0:T(8,128)}, s32[200,512]{1,0:T(8,128)S(1)}, u32[]{:S(2)}, u32[]{:S(2)}) collective-permute-start(s32[200,512]{1,0:T(8,128)} %get-tuple-element.67), channel_id=1, source_target_pairs={{0,16},{8,24},{16,0},{24,8},{1,17},{9,25},{17,1},{25,9},{2,18},{10... | collective-permute-start | bytes 1228808 | tf_op jit(solution)/shard_map/ppermute | solution.py:106
  60.3 21.2 %collective-permute-start.12 = (s32[392,256]{1,0:T(8,128)}, s32[392,256]{1,0:T(8,128)S(1)}, u32[]{:S(2)}, u32[]{:S(2)}) collective-permute-start(s32[392,256]{1,0:T(8,128)} %collective-permute-done.7.refs_3_), channel_id=1, source_target_pairs={{0,8},{8,0},{16,24},{24,16},{1,9},{9,1},{17,25},{25,17},{2,10},{10... | collective-permute-start | bytes 1204232 | tf_op jit(solution)/shard_map/ppermute | solution.py:106
  63.1 45.5 %collective-permute-start.16 = (s32[200,512]{1,0:T(8,128)}, s32[200,512]{1,0:T(8,128)S(1)}, u32[]{:S(2)}, u32[]{:S(2)}) collective-permute-start(s32[200,512]{1,0:T(8,128)} %get-tuple-element.67), channel_id=1, source_target_pairs={{0,8},{8,0},{16,24},{24,16},{1,9},{9,1},{17,25},{25,17},{2,10},{10... | collective-permute-start | bytes 1228808 | tf_op jit(solution)/shard_map/ppermute | solution.py:106
  85.4 23.2 %collective-permute-start.13 = (s32[392,256]{1,0:T(8,128)}, s32[392,256]{1,0:T(8,128)S(1)}, u32[]{:S(2)}, u32[]{:S(2)}) collective-permute-start(s32[392,256]{1,0:T(8,128)} %get-tuple-element.73), channel_id=1, source_target_pairs={{0,2},{1,3},{2,0},{3,1},{4,6},{5,7},{6,4},{7,5},{8,10},{9,11},{10,... | collective-permute-start | bytes 1204232 | tf_op jit(solution)/shard_map/ppermute | solution.py:106
  87.0 21.5 %collective-permute-start.14 = (s32[392,256]{1,0:T(8,128)}, s32[392,256]{1,0:T(8,128)S(1)}, u32[]{:S(2)}, u32[]{:S(2)}) collective-permute-start(s32[392,256]{1,0:T(8,128)} %get-tuple-element.74), channel_id=1, source_target_pairs={{0,4},{1,5},{2,6},{3,7},{4,0},{5,1},{6,2},{7,3},{8,12},{9,13},{10,... | collective-permute-start | bytes 1204232 | tf_op jit(solution)/shard_map/ppermute | solution.py:106
  88.6 20.0 %collective-permute-start.15 = (s32[392,256]{1,0:T(8,128)}, s32[392,256]{1,0:T(8,128)S(1)}, u32[]{:S(2)}, u32[]{:S(2)}) collective-permute-start(s32[392,256]{1,0:T(8,128)} %get-tuple-element.75), channel_id=1, source_target_pairs={{0,6},{1,7},{2,4},{3,5},{4,2},{5,3},{6,0},{7,1},{8,14},{9,15},{10,... | collective-permute-start | bytes 1204232 | tf_op jit(solution)/shard_map/ppermute | solution.py:106
  88.9 19.7 %collective-permute-start.18 = (s32[200,512]{1,0:T(8,128)S(1)}, s32[200,512]{1,0:T(8,128)S(1)}, u32[]{:S(2)}, u32[]{:S(2)}) collective-permute-start(s32[200,512]{1,0:T(8,128)S(1)} %collective-permute-done.17.refs_3_), channel_id=1, source_target_pairs={{0,8},{8,0},{16,24},{24,16},{1,9},{9,1},{17,25},{25,17},{2,10},{10... | collective-permute-start | bytes 1228808 | tf_op jit(solution)/shard_map/ppermute | solution.py:106
  116.0 6.6 %collective-permute-start.19 = (f32[4,512,256]{2,1,0:T(8,128)}, f32[4,512,256]{2,1,0:T(8,128)S(1)}, u32[]{:S(2)}, u32[]{:S(2)}) collective-permute-start(f32[4,512,256]{2,1,0:T(8,128)} %get-tuple-element.81), channel_id=1, source_target_pairs={{0,1},{1,0},{2,3},{3,2},{4,5},{5,4},{6,7},{7,6},{8,9},{9,8},{10,11... | collective-permute-start | bytes 6291464 | tf_op jit(solution)/shard_map/ppermute | solution.py:106
  116.1 13.2 %collective-permute-start.23 = (s32[392,256]{1,0:T(8,128)S(1)}, s32[392,256]{1,0:T(8,128)S(1)}, u32[]{:S(2)}, u32[]{:S(2)}) collective-permute-start(s32[392,256]{1,0:T(8,128)S(1)} %copy-done.5), channel_id=1, source_target_pairs={{0,1},{1,0},{2,3},{3,2},{4,5},{5,4},{6,7},{7,6},{8,9},{9,8},{10,11... | collective-permute-start | bytes 1204232 | tf_op jit(solution)/shard_map/ppermute | solution.py:106
  116.6 14.2 %collective-permute-start.24 = (s32[392,256]{1,0:T(8,128)S(1)}, s32[392,256]{1,0:T(8,128)}, u32[]{:S(2)}, u32[]{:S(2)}) collective-permute-start(s32[392,256]{1,0:T(8,128)S(1)} %collective-permute-done.13.refs_10_), channel_id=1, source_target_pairs={{0,1},{1,0},{2,3},{3,2},{4,5},{5,4},{6,7},{7,6},{8,9},{9,8},{10,11... | collective-permute-start | bytes 1204232 | tf_op jit(solution)/shard_map/ppermute | solution.py:106
  116.6 14.5 %collective-permute-start.25 = (s32[392,256]{1,0:T(8,128)S(1)}, s32[392,256]{1,0:T(8,128)}, u32[]{:S(2)}, u32[]{:S(2)}) collective-permute-start(s32[392,256]{1,0:T(8,128)S(1)} %collective-permute-done.14.refs_11_), channel_id=1, source_target_pairs={{0,1},{1,0},{2,3},{3,2},{4,5},{5,4},{6,7},{7,6},{8,9},{9,8},{10,11... | collective-permute-start | bytes 1204232 | tf_op jit(solution)/shard_map/ppermute | solution.py:106
  117.1 14.1 %collective-permute-start.26 = (s32[392,256]{1,0:T(8,128)S(1)}, s32[392,256]{1,0:T(8,128)}, u32[]{:S(2)}, u32[]{:S(2)}) collective-permute-start(s32[392,256]{1,0:T(8,128)S(1)} %collective-permute-done.15.refs_12_), channel_id=1, source_target_pairs={{0,1},{1,0},{2,3},{3,2},{4,5},{5,4},{6,7},{7,6},{8,9},{9,8},{10,11... | collective-permute-start | bytes 1204232 | tf_op jit(solution)/shard_map/ppermute | solution.py:106
  127.5 21.1 %collective-permute-start.20 = (s32[392,256]{1,0:T(8,128)}, s32[392,256]{1,0:T(8,128)S(1)}, u32[]{:S(2)}, u32[]{:S(2)}) collective-permute-start(s32[392,256]{1,0:T(8,128)} %get-tuple-element.83), channel_id=1, source_target_pairs={{0,2},{1,3},{2,0},{3,1},{4,6},{5,7},{6,4},{7,5},{8,10},{9,11},{10,... | collective-permute-start | bytes 1204232 | tf_op jit(solution)/shard_map/ppermute | solution.py:106
  129.3 19.9 %collective-permute-start.21 = (s32[392,256]{1,0:T(8,128)}, s32[392,256]{1,0:T(8,128)S(1)}, u32[]{:S(2)}, u32[]{:S(2)}) collective-permute-start(s32[392,256]{1,0:T(8,128)} %get-tuple-element.84), channel_id=1, source_target_pairs={{0,4},{1,5},{2,6},{3,7},{4,0},{5,1},{6,2},{7,3},{8,12},{9,13},{10,... | collective-permute-start | bytes 1204232 | tf_op jit(solution)/shard_map/ppermute | solution.py:106
  130.8 18.3 %collective-permute-start.22 = (s32[392,256]{1,0:T(8,128)}, s32[392,256]{1,0:T(8,128)S(1)}, u32[]{:S(2)}, u32[]{:S(2)}) collective-permute-start(s32[392,256]{1,0:T(8,128)} %get-tuple-element.85), channel_id=1, source_target_pairs={{0,6},{1,7},{2,4},{3,5},{4,2},{5,3},{6,0},{7,1},{8,14},{9,15},{10,... | collective-permute-start | bytes 1204232 | tf_op jit(solution)/shard_map/ppermute | solution.py:106
  (17 other events, 113.0 us)
